TPU v7x, 32 devices: a whole 2x2x4 slice. The times are simulated.
32 devices in a mesh: clips: 2 (over y), tiles: 4 (over z), frames: 2 (over x), chan: 2 (over core).
Axes of the slice: x: 2, y: 2, z: 4, core: 2. Of those that a mesh axis runs over, the one named last changes fastest.
Arguments:
- lr_feats: bfloat16 [8, 2, 64, 32, 128], P('clips', 'frames', 'chan', 'tiles'), parts along dimension 0, may hold values from -6 to 6
- flow_prev: int32 [8, 2, 4, 2], P('clips', None, 'tiles'), parts along dimension 0, may hold values from -8 to 8, as said below
- flow_second: int32 [8, 2, 4, 2], P('clips', None, 'tiles'), parts along dimension 0, may hold values from -8 to 8, as said below
- w_join: bfloat16 [9, 64, 192], P(None, 'chan'), may hold values from -0.15625 to 0.15625
- b_join: float32 [64], P('chan'), may hold values from -3 to 3
- w_first: bfloat16 [1, 9, 64, 64], P(None, None, 'chan'), may hold values from -0.25 to 0.25
- b_first: float32 [1, 64], P(None, 'chan'), may hold values from -3 to 3
- w_second: bfloat16 [1, 9, 64, 64], P(None, None, 'chan'), may hold values from -0.25 to 0.25
- b_second: float32 [1, 64], P(None, 'chan'), may hold values from -3 to 3
Outputs:
- hidden: bfloat16 [8, 2, 64, 32, 128], P('clips', 'frames', 'chan', 'tiles'), parts along dimension 0
There are 2 independent parts, one for each index of `clips`. A program takes and returns all parts, laid end to end along the dimension named above; an argument that names none is the same for every part. Nothing has to cross between parts.
Inputs may be any that keep to these rules, and one draw needn't show every extreme that they name: `flow_prev`: both entries (dy, dx) of every block lie in the range; +8 and -8 each occur in every draw. `flow_second`: both entries (dy, dx) of every block lie in the range; +8 and -8 each occur in every draw.
All inputs are finite; a program needn't handle non-finite values.
Results may differ from a plain program's by a relative error of at most 0.012.
Values may be sent and summed in bfloat16 or wider, within the bound.
A program may use at most 64 MiB of HBM per device.

v0:
```python
import jax
import jax.numpy as jnp
from jax import lax
from jax.sharding import PartitionSpec as P

BH = 8


def padded_2(array, sides, width):
    for axis, dim in sides:
        devices, length = (lax.axis_size(axis), array.shape[dim])
        up = [(i, (i + 1) % devices) for i in range(devices - 1)]
        down = [(j, i) for i, j in up]
        last = lax.slice_in_dim(array, length - width, length, axis=dim)
        first = lax.slice_in_dim(array, 0, width, axis=dim)
        before = lax.ppermute(last, axis, up)
        after = lax.ppermute(first, axis, down)
        array = jnp.concatenate([before, array, after], axis=dim)
    return array


def for_sending(array):
    return jax.tree.map(lambda a: a.astype(jnp.bfloat16) if a.dtype == jnp.float32 else a, array)


def shifted(block, axis, distance):
    devices = range(lax.axis_size(axis))
    route = [(i - distance, i) for i in devices if i - distance in devices]
    return lax.ppermute(block, axis, route)


def displace(rimmed, offsets, tile_rows):
    channels = rimmed.shape[0]
    col_count = rimmed.shape[2]
    padded = jnp.pad(rimmed, ((0, 0), (0, 0), (tile_rows, tile_rows)))
    start_row = tile_rows + offsets[0, 0]
    start_col = tile_rows + offsets[0, 1]
    pieces = [lax.dynamic_slice(padded, (0, start_row, start_col), (channels, BH, col_count))]
    return jnp.concatenate(pieces, axis=1)


def convolve_rows(inputs, weights, bias_vec):
    in_count, row_count, col_count = inputs.shape
    rimmed = padded_2(inputs, (("tiles", 1),), 1)
    padded = jnp.pad(rimmed, ((0, 0), (0, 0), (1, 1)))
    total_sum = jnp.zeros((weights.shape[1], row_count * col_count), jnp.float32)
    for tap_index in range(9):
        tap_row = tap_index // 3
        tap_col = tap_index % 3
        window = padded[:, tap_row : tap_row + row_count, tap_col : tap_col + col_count].reshape(
            in_count, row_count * col_count
        )
        total_sum = total_sum + jnp.dot(
            weights[tap_index], window, preferred_element_type=jnp.float32
        )
    return total_sum.reshape(-1, row_count, col_count) + bias_vec[:, None, None]


def block_conv(own_part, weights, bias_vec):
    whole_input = lax.all_gather(own_part, "chan", axis=0, tiled=True)
    return convolve_rows(whole_input, weights, bias_vec)


def refine(current, warped_one, warped_two, w_join, b_join, w_first, b_first, w_second, b_second):
    full_current, full_one, full_two = (
        lax.all_gather(current, "chan", axis=0, tiled=True),
        lax.all_gather(warped_one, "chan", axis=0, tiled=True),
        lax.all_gather(warped_two, "chan", axis=0, tiled=True),
    )
    stacked = jnp.concatenate([full_current, full_one, full_two], axis=0)
    joined_sum = convolve_rows(stacked, w_join, b_join)
    joined_state = jnp.where(joined_sum > 0, joined_sum, 0.1 * joined_sum).astype(jnp.bfloat16)
    inner_act = jnp.maximum(block_conv(joined_state, w_first[0], b_first[0]), 0.0).astype(
        jnp.bfloat16
    )
    joined_state = (
        joined_state.astype(jnp.float32) + block_conv(inner_act, w_second[0], b_second[0])
    ).astype(jnp.bfloat16)
    return joined_state


def shards(lr_feats, flow_prev, flow_second, w_join, b_join, w_first, b_first, w_second, b_second):
    segments = lr_feats.shape[0]
    tile_rows = lr_feats.shape[3]
    frames_all = flow_prev.shape[1]
    owners = lax.axis_size("frames")
    position = lax.axis_index("frames")
    blank_feat = jnp.zeros(lr_feats.shape[2:], lr_feats.dtype)

    def advance(turn_index, carried):
        results, first_in, second_in, second_wait = carried
        segment = turn_index - position
        is_valid = (segment >= 0) & (segment < segments)
        seg_clip = jnp.clip(segment, 0, segments - 1)
        current = lax.dynamic_index_in_dim(lr_feats, seg_clip, 0, keepdims=False)[0]
        fresh_state = refine(
            current, first_in, second_in, w_join, b_join, w_first, b_first, w_second, b_second
        )
        kept_slice = lax.dynamic_index_in_dim(results, seg_clip, 0, keepdims=True)
        chosen = jnp.where(is_valid, fresh_state[None, None], kept_slice)
        results = lax.dynamic_update_index_in_dim(results, chosen[0], seg_clip, 0)
        rimmed_own = padded_2(fresh_state, (("tiles", 1),), tile_rows)
        frame_next = jnp.minimum(position + 1, frames_all - 1)
        frame_after = jnp.minimum(position + 2, frames_all - 1)
        ahead_one = displace(rimmed_own, flow_prev[seg_clip, frame_next], tile_rows)
        ahead_two = displace(rimmed_own, flow_second[seg_clip, frame_after], tile_rows)
        first_next = shifted(for_sending(ahead_one), "frames", 1).astype(ahead_one.dtype)
        wait_next = shifted(for_sending(ahead_two), "frames", 2).astype(ahead_two.dtype)
        return (results, first_next, second_wait, wait_next)

    initial = (jnp.zeros_like(lr_feats), blank_feat, blank_feat, blank_feat)
    results, first_in, second_in, second_wait = lax.fori_loop(
        0, segments + owners - 1, advance, initial
    )
    return results


def solution(mesh):
    in_specs = (
        P("clips", "frames", "chan", "tiles", None),
        P("clips", None, "tiles", None),
        P("clips", None, "tiles", None),
        P(None, "chan", None),
        P("chan"),
        P(None, None, "chan", None),
        P(None, "chan"),
        P(None, None, "chan", None),
        P(None, "chan"),
    )
    out_specs = P("clips", "frames", "chan", "tiles", None)
    return jax.shard_map(shards, mesh=mesh, in_specs=in_specs, out_specs=out_specs, check_vma=False)
```

profile of v0, /device:TPU:0, one launch (start us, length us, event | category | flops | bytes accessed | tf_op | source)
XLA Modules:
  0.0 324.6 jit_solution(14142174977703277329)
XLA Ops:
  1.6 322.3 %while.22 = (s32[]{:T(128)}, bf16[4,1,32,8,128]{4,3,2,1,0:T(8,128)(2,1)S(1)}, bf16[32,8,128]{2,1,0:T(8,128)(2,1)S(1)}, bf16[32,8,128]{2,1,0:T(8,128)(2,1)S(1)}, ...) while((s32[]{:T(128)}, ...), condition=%wide.region_1.2_spmd, body=%wide.region_0.1_spmd.sunk | while | flops 202819072 | bytes 31908440 | solution.py:112
  2.5 2.0 all-gather.2
  4.5 1.9 all_gather.59
  6.4 1.9 all_gather.60
  9.8 5.5 %collective-permute-start.1 = (bf16[192,1,128]{2,1,0:T(2,128)(2,1)S(1)}, bf16[192,1,128]{2,1,0:T(2,128)(2,1)S(1)}, u32[]{:S(2)}, u32[]{:S(2)}) collective-permute-start(bf16[192,1,128]{2,1,0:T(2,128)(2,1)S(1)} %get-tuple-element.690), channel_id=1, source_target_pairs={{0,4},{4,8},{8,12},{1,5},{5,9},{9,13},{2,6},{6,10},{10,14},{3,7},{... | collective-permute-start | bytes 147464 | tf_op jit(solution)/shard_map/while/body/eval_jaxpr/ppermute | solution.py:16
  17.6 4.1 %select_maximum_fusion.6 = bf16[192,10,130]{2,1,0:T(8,128)(2,1)S(1)} fusion(bf16[192,1,128]{2,1,0:T(2,128)(2,1)S(1)} %collective-permute-done, bf16[192,1,128]{2,1,0:T(2,128)(2,1)S(1)} %collective-permute-done.1, bf16[64,8,128]{2,1,0:T(8,128)(2,1)S(1)} %all_gather.59, bf16[64,8,128]{2,1,0:T(8,128)(2,1)S(1)} %all_gather.60, ...), kind=kLoop, calls=%fused_computation.5.clone.1 | loop fusion | flops 4492800 | bytes 990720 | tf_op jit(solution)/shard_map/while/body/eval_jaxpr/concatenate | solution.py:18
  24.8 1.9 all_gather.61
  28.1 5.0 %collective-permute-start.3 = (bf16[64,1,128]{2,1,0:T(2,128)(2,1)S(1)}, bf16[64,1,128]{2,1,0:T(2,128)(2,1)S(1)}, u32[]{:S(2)}, u32[]{:S(2)}) collective-permute-start(bf16[64,1,128]{2,1,0:T(2,128)(2,1)S(1)} %get-tuple-element.700), channel_id=1, source_target_pairs={{0,4},{4,8},{8,12},{1,5},{5,9},{9,13},{2,6},{6,10},{10,14},{3,7},{... | collective-permute-start | bytes 49160 | tf_op jit(solution)/shard_map/while/body/eval_jaxpr/ppermute | solution.py:16
  37.1 1.9 all_gather.62
  40.4 4.9 %collective-permute-start.5 = (bf16[64,1,128]{2,1,0:T(2,128)(2,1)S(1)}, bf16[64,1,128]{2,1,0:T(2,128)(2,1)S(1)}, u32[]{:S(2)}, u32[]{:S(2)}) collective-permute-start(bf16[64,1,128]{2,1,0:T(2,128)(2,1)S(1)} %get-tuple-element.710), channel_id=1, source_target_pairs={{0,4},{4,8},{8,12},{1,5},{5,9},{9,13},{2,6},{6,10},{10,14},{3,7},{... | collective-permute-start | bytes 49160 | tf_op jit(solution)/shard_map/while/body/eval_jaxpr/ppermute | solution.py:16
  50.8 4.6 %collective-permute-start.7 = (bf16[32,8,128]{2,1,0:T(8,128)(2,1)S(1)}, bf16[32,8,128]{2,1,0:T(8,128)(2,1)S(1)}, u32[]{:S(2)}, u32[]{:S(2)}) collective-permute-start(bf16[32,8,128]{2,1,0:T(8,128)(2,1)S(1)} %fusion.295), channel_id=1, source_target_pairs={{0,4},{4,8},{8,12},{1,5},{5,9},{9,13},{2,6},{6,10},{10,14},{3,7},{... | collective-permute-start | bytes 196616 | tf_op jit(solution)/shard_map/while/body/eval_jaxpr/ppermute | solution.py:16
  60.9 3.6 %collective-permute-start.8 = (bf16[32,8,128]{2,1,0:T(8,128)(2,1)S(1)}, bf16[32,8,128]{2,1,0:T(8,128)(2,1)S(1)}, u32[]{:S(2)}, u32[]{:S(2)}) collective-permute-start(bf16[32,8,128]{2,1,0:T(8,128)(2,1)S(1)} %get-tuple-element.725), channel_id=1, source_target_pairs={{0,2},{1,3},{4,6},{5,7},{8,10},{9,11},{12,14},{13,15},{16,18},{17,... | collective-permute-start | bytes 196616 | tf_op jit(solution)/shard_map/while/body/eval_jaxpr/ppermute | solution.py:29
  69.1 1.9 all_gather.59
  71.0 1.9 all_gather.60
  74.4 4.6 %collective-permute-start.1 = (bf16[192,1,128]{2,1,0:T(2,128)(2,1)S(1)}, bf16[192,1,128]{2,1,0:T(2,128)(2,1)S(1)}, u32[]{:S(2)}, u32[]{:S(2)}) collective-permute-start(bf16[192,1,128]{2,1,0:T(2,128)(2,1)S(1)} %get-tuple-element.690), channel_id=1, source_target_pairs={{0,4},{4,8},{8,12},{1,5},{5,9},{9,13},{2,6},{6,10},{10,14},{3,7},{... | collective-permute-start | bytes 147464 | tf_op jit(solution)/shard_map/while/body/eval_jaxpr/ppermute | solution.py:16
  81.3 4.1 %select_maximum_fusion.6 = bf16[192,10,130]{2,1,0:T(8,128)(2,1)S(1)} fusion(bf16[192,1,128]{2,1,0:T(2,128)(2,1)S(1)} %collective-permute-done, bf16[192,1,128]{2,1,0:T(2,128)(2,1)S(1)} %collective-permute-done.1, bf16[64,8,128]{2,1,0:T(8,128)(2,1)S(1)} %all_gather.59, bf16[64,8,128]{2,1,0:T(8,128)(2,1)S(1)} %all_gather.60, ...), kind=kLoop, calls=%fused_computation.5.clone.1 | loop fusion | flops 4492800 | bytes 990720 | tf_op jit(solution)/shard_map/while/body/eval_jaxpr/concatenate | solution.py:18
  88.6 1.9 all_gather.61
  91.8 5.0 %collective-permute-start.3 = (bf16[64,1,128]{2,1,0:T(2,128)(2,1)S(1)}, bf16[64,1,128]{2,1,0:T(2,128)(2,1)S(1)}, u32[]{:S(2)}, u32[]{:S(2)}) collective-permute-start(bf16[64,1,128]{2,1,0:T(2,128)(2,1)S(1)} %get-tuple-element.700), channel_id=1, source_target_pairs={{0,4},{4,8},{8,12},{1,5},{5,9},{9,13},{2,6},{6,10},{10,14},{3,7},{... | collective-permute-start | bytes 49160 | tf_op jit(solution)/shard_map/while/body/eval_jaxpr/ppermute | solution.py:16
  100.8 1.9 all_gather.62
  104.1 4.9 %collective-permute-start.5 = (bf16[64,1,128]{2,1,0:T(2,128)(2,1)S(1)}, bf16[64,1,128]{2,1,0:T(2,128)(2,1)S(1)}, u32[]{:S(2)}, u32[]{:S(2)}) collective-permute-start(bf16[64,1,128]{2,1,0:T(2,128)(2,1)S(1)} %get-tuple-element.710), channel_id=1, source_target_pairs={{0,4},{4,8},{8,12},{1,5},{5,9},{9,13},{2,6},{6,10},{10,14},{3,7},{... | collective-permute-start | bytes 49160 | tf_op jit(solution)/shard_map/while/body/eval_jaxpr/ppermute | solution.py:16
  114.5 4.6 %collective-permute-start.7 = (bf16[32,8,128]{2,1,0:T(8,128)(2,1)S(1)}, bf16[32,8,128]{2,1,0:T(8,128)(2,1)S(1)}, u32[]{:S(2)}, u32[]{:S(2)}) collective-permute-start(bf16[32,8,128]{2,1,0:T(8,128)(2,1)S(1)} %fusion.295), channel_id=1, source_target_pairs={{0,4},{4,8},{8,12},{1,5},{5,9},{9,13},{2,6},{6,10},{10,14},{3,7},{... | collective-permute-start | bytes 196616 | tf_op jit(solution)/shard_map/while/body/eval_jaxpr/ppermute | solution.py:16
  124.6 4.3 %collective-permute-start.8 = (bf16[32,8,128]{2,1,0:T(8,128)(2,1)S(1)}, bf16[32,8,128]{2,1,0:T(8,128)(2,1)S(1)}, u32[]{:S(2)}, u32[]{:S(2)}) collective-permute-start(bf16[32,8,128]{2,1,0:T(8,128)(2,1)S(1)} %get-tuple-element.725), channel_id=1, source_target_pairs={{0,2},{1,3},{4,6},{5,7},{8,10},{9,11},{12,14},{13,15},{16,18},{17,... | collective-permute-start | bytes 196616 | tf_op jit(solution)/shard_map/while/body/eval_jaxpr/ppermute | solution.py:29
  133.5 1.9 all_gather.59
  135.4 1.9 all_gather.60
  138.8 4.6 %collective-permute-start.1 = (bf16[192,1,128]{2,1,0:T(2,128)(2,1)S(1)}, bf16[192,1,128]{2,1,0:T(2,128)(2,1)S(1)}, u32[]{:S(2)}, u32[]{:S(2)}) collective-permute-start(bf16[192,1,128]{2,1,0:T(2,128)(2,1)S(1)} %get-tuple-element.690), channel_id=1, source_target_pairs={{0,4},{4,8},{8,12},{1,5},{5,9},{9,13},{2,6},{6,10},{10,14},{3,7},{... | collective-permute-start | bytes 147464 | tf_op jit(solution)/shard_map/while/body/eval_jaxpr/ppermute | solution.py:16
  145.7 4.1 %select_maximum_fusion.6 = bf16[192,10,130]{2,1,0:T(8,128)(2,1)S(1)} fusion(bf16[192,1,128]{2,1,0:T(2,128)(2,1)S(1)} %collective-permute-done, bf16[192,1,128]{2,1,0:T(2,128)(2,1)S(1)} %collective-permute-done.1, bf16[64,8,128]{2,1,0:T(8,128)(2,1)S(1)} %all_gather.59, bf16[64,8,128]{2,1,0:T(8,128)(2,1)S(1)} %all_gather.60, ...), kind=kLoop, calls=%fused_computation.5.clone.1 | loop fusion | flops 4492800 | bytes 990720 | tf_op jit(solution)/shard_map/while/body/eval_jaxpr/concatenate | solution.py:18
  152.9 1.9 all_gather.61
  156.2 5.0 %collective-permute-start.3 = (bf16[64,1,128]{2,1,0:T(2,128)(2,1)S(1)}, bf16[64,1,128]{2,1,0:T(2,128)(2,1)S(1)}, u32[]{:S(2)}, u32[]{:S(2)}) collective-permute-start(bf16[64,1,128]{2,1,0:T(2,128)(2,1)S(1)} %get-tuple-element.700), channel_id=1, source_target_pairs={{0,4},{4,8},{8,12},{1,5},{5,9},{9,13},{2,6},{6,10},{10,14},{3,7},{... | collective-permute-start | bytes 49160 | tf_op jit(solution)/shard_map/while/body/eval_jaxpr/ppermute | solution.py:16
  165.2 1.9 all_gather.62
  168.5 4.9 %collective-permute-start.5 = (bf16[64,1,128]{2,1,0:T(2,128)(2,1)S(1)}, bf16[64,1,128]{2,1,0:T(2,128)(2,1)S(1)}, u32[]{:S(2)}, u32[]{:S(2)}) collective-permute-start(bf16[64,1,128]{2,1,0:T(2,128)(2,1)S(1)} %get-tuple-element.710), channel_id=1, source_target_pairs={{0,4},{4,8},{8,12},{1,5},{5,9},{9,13},{2,6},{6,10},{10,14},{3,7},{... | collective-permute-start | bytes 49160 | tf_op jit(solution)/shard_map/while/body/eval_jaxpr/ppermute | solution.py:16
  178.9 4.6 %collective-permute-start.7 = (bf16[32,8,128]{2,1,0:T(8,128)(2,1)S(1)}, bf16[32,8,128]{2,1,0:T(8,128)(2,1)S(1)}, u32[]{:S(2)}, u32[]{:S(2)}) collective-permute-start(bf16[32,8,128]{2,1,0:T(8,128)(2,1)S(1)} %fusion.295), channel_id=1, source_target_pairs={{0,4},{4,8},{8,12},{1,5},{5,9},{9,13},{2,6},{6,10},{10,14},{3,7},{... | collective-permute-start | bytes 196616 | tf_op jit(solution)/shard_map/while/body/eval_jaxpr/ppermute | solution.py:16
  189.0 4.3 %collective-permute-start.8 = (bf16[32,8,128]{2,1,0:T(8,128)(2,1)S(1)}, bf16[32,8,128]{2,1,0:T(8,128)(2,1)S(1)}, u32[]{:S(2)}, u32[]{:S(2)}) collective-permute-start(bf16[32,8,128]{2,1,0:T(8,128)(2,1)S(1)} %get-tuple-element.725), channel_id=1, source_target_pairs={{0,2},{1,3},{4,6},{5,7},{8,10},{9,11},{12,14},{13,15},{16,18},{17,... | collective-permute-start | bytes 196616 | tf_op jit(solution)/shard_map/while/body/eval_jaxpr/ppermute | solution.py:29
  203.1 4.6 %collective-permute-start.1 = (bf16[192,1,128]{2,1,0:T(2,128)(2,1)S(1)}, bf16[192,1,128]{2,1,0:T(2,128)(2,1)S(1)}, u32[]{:S(2)}, u32[]{:S(2)}) collective-permute-start(bf16[192,1,128]{2,1,0:T(2,128)(2,1)S(1)} %get-tuple-element.690), channel_id=1, source_target_pairs={{0,4},{4,8},{8,12},{1,5},{5,9},{9,13},{2,6},{6,10},{10,14},{3,7},{... | collective-permute-start | bytes 147464 | tf_op jit(solution)/shard_map/while/body/eval_jaxpr/ppermute | solution.py:16
  210.1 4.1 %select_maximum_fusion.6 = bf16[192,10,130]{2,1,0:T(8,128)(2,1)S(1)} fusion(bf16[192,1,128]{2,1,0:T(2,128)(2,1)S(1)} %collective-permute-done, bf16[192,1,128]{2,1,0:T(2,128)(2,1)S(1)} %collective-permute-done.1, bf16[64,8,128]{2,1,0:T(8,128)(2,1)S(1)} %all_gather.59, bf16[64,8,128]{2,1,0:T(8,128)(2,1)S(1)} %all_gather.60, ...), kind=kLoop, calls=%fused_computation.5.clone.1 | loop fusion | flops 4492800 | bytes 990720 | tf_op jit(solution)/shard_map/while/body/eval_jaxpr/concatenate | solution.py:18
  217.3 1.9 all_gather.61
  220.6 5.0 %collective-permute-start.3 = (bf16[64,1,128]{2,1,0:T(2,128)(2,1)S(1)}, bf16[64,1,128]{2,1,0:T(2,128)(2,1)S(1)}, u32[]{:S(2)}, u32[]{:S(2)}) collective-permute-start(bf16[64,1,128]{2,1,0:T(2,128)(2,1)S(1)} %get-tuple-element.700), channel_id=1, source_target_pairs={{0,4},{4,8},{8,12},{1,5},{5,9},{9,13},{2,6},{6,10},{10,14},{3,7},{... | collective-permute-start | bytes 49160 | tf_op jit(solution)/shard_map/while/body/eval_jaxpr/ppermute | solution.py:16
  229.6 1.9 all_gather.62
  232.9 4.9 %collective-permute-start.5 = (bf16[64,1,128]{2,1,0:T(2,128)(2,1)S(1)}, bf16[64,1,128]{2,1,0:T(2,128)(2,1)S(1)}, u32[]{:S(2)}, u32[]{:S(2)}) collective-permute-start(bf16[64,1,128]{2,1,0:T(2,128)(2,1)S(1)} %get-tuple-element.710), channel_id=1, source_target_pairs={{0,4},{4,8},{8,12},{1,5},{5,9},{9,13},{2,6},{6,10},{10,14},{3,7},{... | collective-permute-start | bytes 49160 | tf_op jit(solution)/shard_map/while/body/eval_jaxpr/ppermute | solution.py:16
  243.3 4.6 %collective-permute-start.7 = (bf16[32,8,128]{2,1,0:T(8,128)(2,1)S(1)}, bf16[32,8,128]{2,1,0:T(8,128)(2,1)S(1)}, u32[]{:S(2)}, u32[]{:S(2)}) collective-permute-start(bf16[32,8,128]{2,1,0:T(8,128)(2,1)S(1)} %fusion.295), channel_id=1, source_target_pairs={{0,4},{4,8},{8,12},{1,5},{5,9},{9,13},{2,6},{6,10},{10,14},{3,7},{... | collective-permute-start | bytes 196616 | tf_op jit(solution)/shard_map/while/body/eval_jaxpr/ppermute | solution.py:16
  253.4 4.3 %collective-permute-start.8 = (bf16[32,8,128]{2,1,0:T(8,128)(2,1)S(1)}, bf16[32,8,128]{2,1,0:T(8,128)(2,1)S(1)}, u32[]{:S(2)}, u32[]{:S(2)}) collective-permute-start(bf16[32,8,128]{2,1,0:T(8,128)(2,1)S(1)} %get-tuple-element.725), channel_id=1, source_target_pairs={{0,2},{1,3},{4,6},{5,7},{8,10},{9,11},{12,14},{13,15},{16,18},{17,... | collective-permute-start | bytes 196616 | tf_op jit(solution)/shard_map/while/body/eval_jaxpr/ppermute | solution.py:29
  267.5 4.6 %collective-permute-start.1 = (bf16[192,1,128]{2,1,0:T(2,128)(2,1)S(1)}, bf16[192,1,128]{2,1,0:T(2,128)(2,1)S(1)}, u32[]{:S(2)}, u32[]{:S(2)}) collective-permute-start(bf16[192,1,128]{2,1,0:T(2,128)(2,1)S(1)} %get-tuple-element.690), channel_id=1, source_target_pairs={{0,4},{4,8},{8,12},{1,5},{5,9},{9,13},{2,6},{6,10},{10,14},{3,7},{... | collective-permute-start | bytes 147464 | tf_op jit(solution)/shard_map/while/body/eval_jaxpr/ppermute | solution.py:16
  274.4 4.1 %select_maximum_fusion.6 = bf16[192,10,130]{2,1,0:T(8,128)(2,1)S(1)} fusion(bf16[192,1,128]{2,1,0:T(2,128)(2,1)S(1)} %collective-permute-done, bf16[192,1,128]{2,1,0:T(2,128)(2,1)S(1)} %collective-permute-done.1, bf16[64,8,128]{2,1,0:T(8,128)(2,1)S(1)} %all_gather.59, bf16[64,8,128]{2,1,0:T(8,128)(2,1)S(1)} %all_gather.60, ...), kind=kLoop, calls=%fused_computation.5.clone.1 | loop fusion | flops 4492800 | bytes 990720 | tf_op jit(solution)/shard_map/while/body/eval_jaxpr/concatenate | solution.py:18
  281.7 1.9 all_gather.61
  284.9 5.0 %collective-permute-start.3 = (bf16[64,1,128]{2,1,0:T(2,128)(2,1)S(1)}, bf16[64,1,128]{2,1,0:T(2,128)(2,1)S(1)}, u32[]{:S(2)}, u32[]{:S(2)}) collective-permute-start(bf16[64,1,128]{2,1,0:T(2,128)(2,1)S(1)} %get-tuple-element.700), channel_id=1, source_target_pairs={{0,4},{4,8},{8,12},{1,5},{5,9},{9,13},{2,6},{6,10},{10,14},{3,7},{... | collective-permute-start | bytes 49160 | tf_op jit(solution)/shard_map/while/body/eval_jaxpr/ppermute | solution.py:16
  294.0 1.9 all_gather.62
  297.2 4.9 %collective-permute-start.5 = (bf16[64,1,128]{2,1,0:T(2,128)(2,1)S(1)}, bf16[64,1,128]{2,1,0:T(2,128)(2,1)S(1)}, u32[]{:S(2)}, u32[]{:S(2)}) collective-permute-start(bf16[64,1,128]{2,1,0:T(2,128)(2,1)S(1)} %get-tuple-element.710), channel_id=1, source_target_pairs={{0,4},{4,8},{8,12},{1,5},{5,9},{9,13},{2,6},{6,10},{10,14},{3,7},{... | collective-permute-start | bytes 49160 | tf_op jit(solution)/shard_map/while/body/eval_jaxpr/ppermute | solution.py:16
  307.7 4.6 %collective-permute-start.7 = (bf16[32,8,128]{2,1,0:T(8,128)(2,1)S(1)}, bf16[32,8,128]{2,1,0:T(8,128)(2,1)S(1)}, u32[]{:S(2)}, u32[]{:S(2)}) collective-permute-start(bf16[32,8,128]{2,1,0:T(8,128)(2,1)S(1)} %fusion.295), channel_id=1, source_target_pairs={{0,4},{4,8},{8,12},{1,5},{5,9},{9,13},{2,6},{6,10},{10,14},{3,7},{... | collective-permute-start | bytes 196616 | tf_op jit(solution)/shard_map/while/body/eval_jaxpr/ppermute | solution.py:16
  317.8 4.3 %collective-permute-start.8 = (bf16[32,8,128]{2,1,0:T(8,128)(2,1)S(1)}, bf16[32,8,128]{2,1,0:T(8,128)(2,1)S(1)}, u32[]{:S(2)}, u32[]{:S(2)}) collective-permute-start(bf16[32,8,128]{2,1,0:T(8,128)(2,1)S(1)} %get-tuple-element.725), channel_id=1, source_target_pairs={{0,2},{1,3},{4,6},{5,7},{8,10},{9,11},{12,14},{13,15},{16,18},{17,... | collective-permute-start | bytes 196616 | tf_op jit(solution)/shard_map/while/body/eval_jaxpr/ppermute | solution.py:29
  (416 shorter events, 127.9 us)
Async XLA Ops:
  8.5 7.9 %collective-permute-start = (bf16[192,1,128]{2,1,0:T(2,128)(2,1)S(1)}, bf16[192,1,128]{2,1,0:T(2,128)(2,1)S(1)}, u32[]{:S(2)}, u32[]{:S(2)}) collective-permute-start(bf16[192,1,128]{2,1,0:T(2,128)(2,1)S(1)} %get-tuple-element.689), channel_id=1, source_target_pairs={{4,0},{8,4},{12,8},{5,1},{9,5},{13,9},{6,2},{10,6},{14,10},{7,3},{... | collective-permute-start | bytes 147464 | tf_op jit(solution)/shard_map/while/body/eval_jaxpr/ppermute | solution.py:17
  9.8 7.8 %collective-permute-start.1 = (bf16[192,1,128]{2,1,0:T(2,128)(2,1)S(1)}, bf16[192,1,128]{2,1,0:T(2,128)(2,1)S(1)}, u32[]{:S(2)}, u32[]{:S(2)}) collective-permute-start(bf16[192,1,128]{2,1,0:T(2,128)(2,1)S(1)} %get-tuple-element.690), channel_id=1, source_target_pairs={{0,4},{4,8},{8,12},{1,5},{5,9},{9,13},{2,6},{6,10},{10,14},{3,7},{... | collective-permute-start | bytes 147464 | tf_op jit(solution)/shard_map/while/body/eval_jaxpr/ppermute | solution.py:16
  26.8 6.3 %collective-permute-start.2 = (bf16[64,1,128]{2,1,0:T(2,128)(2,1)S(1)}, bf16[64,1,128]{2,1,0:T(2,128)(2,1)S(1)}, u32[]{:S(2)}, u32[]{:S(2)}) collective-permute-start(bf16[64,1,128]{2,1,0:T(2,128)(2,1)S(1)} %get-tuple-element.699), channel_id=1, source_target_pairs={{4,0},{8,4},{12,8},{5,1},{9,5},{13,9},{6,2},{10,6},{14,10},{7,3},{... | collective-permute-start | bytes 49160 | tf_op jit(solution)/shard_map/while/body/eval_jaxpr/ppermute | solution.py:17
  28.1 6.6 %collective-permute-start.3 = (bf16[64,1,128]{2,1,0:T(2,128)(2,1)S(1)}, bf16[64,1,128]{2,1,0:T(2,128)(2,1)S(1)}, u32[]{:S(2)}, u32[]{:S(2)}) collective-permute-start(bf16[64,1,128]{2,1,0:T(2,128)(2,1)S(1)} %get-tuple-element.700), channel_id=1, source_target_pairs={{0,4},{4,8},{8,12},{1,5},{5,9},{9,13},{2,6},{6,10},{10,14},{3,7},{... | collective-permute-start | bytes 49160 | tf_op jit(solution)/shard_map/while/body/eval_jaxpr/ppermute | solution.py:16
  39.1 7.9 %collective-permute-start.4 = (bf16[64,1,128]{2,1,0:T(2,128)(2,1)S(1)}, bf16[64,1,128]{2,1,0:T(2,128)(2,1)S(1)}, u32[]{:S(2)}, u32[]{:S(2)}) collective-permute-start(bf16[64,1,128]{2,1,0:T(2,128)(2,1)S(1)} %get-tuple-element.709), channel_id=1, source_target_pairs={{4,0},{8,4},{12,8},{5,1},{9,5},{13,9},{6,2},{10,6},{14,10},{7,3},{... | collective-permute-start | bytes 49160 | tf_op jit(solution)/shard_map/while/body/eval_jaxpr/ppermute | solution.py:17
  40.4 6.6 %collective-permute-start.5 = (bf16[64,1,128]{2,1,0:T(2,128)(2,1)S(1)}, bf16[64,1,128]{2,1,0:T(2,128)(2,1)S(1)}, u32[]{:S(2)}, u32[]{:S(2)}) collective-permute-start(bf16[64,1,128]{2,1,0:T(2,128)(2,1)S(1)} %get-tuple-element.710), channel_id=1, source_target_pairs={{0,4},{4,8},{8,12},{1,5},{5,9},{9,13},{2,6},{6,10},{10,14},{3,7},{... | collective-permute-start | bytes 49160 | tf_op jit(solution)/shard_map/while/body/eval_jaxpr/ppermute | solution.py:16
  49.5 10.3 %collective-permute-start.6 = (bf16[32,8,128]{2,1,0:T(8,128)(2,1)S(1)}, bf16[32,8,128]{2,1,0:T(8,128)(2,1)S(1)}, u32[]{:S(2)}, u32[]{:S(2)}) collective-permute-start(bf16[32,8,128]{2,1,0:T(8,128)(2,1)S(1)} %fusion.295), channel_id=1, source_target_pairs={{4,0},{8,4},{12,8},{5,1},{9,5},{13,9},{6,2},{10,6},{14,10},{7,3},{... | collective-permute-start | bytes 196616 | tf_op jit(solution)/shard_map/while/body/eval_jaxpr/ppermute | solution.py:17
  50.8 9.1 %collective-permute-start.7 = (bf16[32,8,128]{2,1,0:T(8,128)(2,1)S(1)}, bf16[32,8,128]{2,1,0:T(8,128)(2,1)S(1)}, u32[]{:S(2)}, u32[]{:S(2)}) collective-permute-start(bf16[32,8,128]{2,1,0:T(8,128)(2,1)S(1)} %fusion.295), channel_id=1, source_target_pairs={{0,4},{4,8},{8,12},{1,5},{5,9},{9,13},{2,6},{6,10},{10,14},{3,7},{... | collective-permute-start | bytes 196616 | tf_op jit(solution)/shard_map/while/body/eval_jaxpr/ppermute | solution.py:16
  60.9 5.5 %collective-permute-start.8 = (bf16[32,8,128]{2,1,0:T(8,128)(2,1)S(1)}, bf16[32,8,128]{2,1,0:T(8,128)(2,1)S(1)}, u32[]{:S(2)}, u32[]{:S(2)}) collective-permute-start(bf16[32,8,128]{2,1,0:T(8,128)(2,1)S(1)} %get-tuple-element.725), channel_id=1, source_target_pairs={{0,2},{1,3},{4,6},{5,7},{8,10},{9,11},{12,14},{13,15},{16,18},{17,... | collective-permute-start | bytes 196616 | tf_op jit(solution)/shard_map/while/body/eval_jaxpr/ppermute | solution.py:29
  73.1 7.0 %collective-permute-start = (bf16[192,1,128]{2,1,0:T(2,128)(2,1)S(1)}, bf16[192,1,128]{2,1,0:T(2,128)(2,1)S(1)}, u32[]{:S(2)}, u32[]{:S(2)}) collective-permute-start(bf16[192,1,128]{2,1,0:T(2,128)(2,1)S(1)} %get-tuple-element.689), channel_id=1, source_target_pairs={{4,0},{8,4},{12,8},{5,1},{9,5},{13,9},{6,2},{10,6},{14,10},{7,3},{... | collective-permute-start | bytes 147464 | tf_op jit(solution)/shard_map/while/body/eval_jaxpr/ppermute | solution.py:17
  74.4 6.9 %collective-permute-start.1 = (bf16[192,1,128]{2,1,0:T(2,128)(2,1)S(1)}, bf16[192,1,128]{2,1,0:T(2,128)(2,1)S(1)}, u32[]{:S(2)}, u32[]{:S(2)}) collective-permute-start(bf16[192,1,128]{2,1,0:T(2,128)(2,1)S(1)} %get-tuple-element.690), channel_id=1, source_target_pairs={{0,4},{4,8},{8,12},{1,5},{5,9},{9,13},{2,6},{6,10},{10,14},{3,7},{... | collective-permute-start | bytes 147464 | tf_op jit(solution)/shard_map/while/body/eval_jaxpr/ppermute | solution.py:16
  90.5 6.3 %collective-permute-start.2 = (bf16[64,1,128]{2,1,0:T(2,128)(2,1)S(1)}, bf16[64,1,128]{2,1,0:T(2,128)(2,1)S(1)}, u32[]{:S(2)}, u32[]{:S(2)}) collective-permute-start(bf16[64,1,128]{2,1,0:T(2,128)(2,1)S(1)} %get-tuple-element.699), channel_id=1, source_target_pairs={{4,0},{8,4},{12,8},{5,1},{9,5},{13,9},{6,2},{10,6},{14,10},{7,3},{... | collective-permute-start | bytes 49160 | tf_op jit(solution)/shard_map/while/body/eval_jaxpr/ppermute | solution.py:17
  91.8 6.6 %collective-permute-start.3 = (bf16[64,1,128]{2,1,0:T(2,128)(2,1)S(1)}, bf16[64,1,128]{2,1,0:T(2,128)(2,1)S(1)}, u32[]{:S(2)}, u32[]{:S(2)}) collective-permute-start(bf16[64,1,128]{2,1,0:T(2,128)(2,1)S(1)} %get-tuple-element.700), channel_id=1, source_target_pairs={{0,4},{4,8},{8,12},{1,5},{5,9},{9,13},{2,6},{6,10},{10,14},{3,7},{... | collective-permute-start | bytes 49160 | tf_op jit(solution)/shard_map/while/body/eval_jaxpr/ppermute | solution.py:16
  102.8 7.9 %collective-permute-start.4 = (bf16[64,1,128]{2,1,0:T(2,128)(2,1)S(1)}, bf16[64,1,128]{2,1,0:T(2,128)(2,1)S(1)}, u32[]{:S(2)}, u32[]{:S(2)}) collective-permute-start(bf16[64,1,128]{2,1,0:T(2,128)(2,1)S(1)} %get-tuple-element.709), channel_id=1, source_target_pairs={{4,0},{8,4},{12,8},{5,1},{9,5},{13,9},{6,2},{10,6},{14,10},{7,3},{... | collective-permute-start | bytes 49160 | tf_op jit(solution)/shard_map/while/body/eval_jaxpr/ppermute | solution.py:17
  104.1 6.6 %collective-permute-start.5 = (bf16[64,1,128]{2,1,0:T(2,128)(2,1)S(1)}, bf16[64,1,128]{2,1,0:T(2,128)(2,1)S(1)}, u32[]{:S(2)}, u32[]{:S(2)}) collective-permute-start(bf16[64,1,128]{2,1,0:T(2,128)(2,1)S(1)} %get-tuple-element.710), channel_id=1, source_target_pairs={{0,4},{4,8},{8,12},{1,5},{5,9},{9,13},{2,6},{6,10},{10,14},{3,7},{... | collective-permute-start | bytes 49160 | tf_op jit(solution)/shard_map/while/body/eval_jaxpr/ppermute | solution.py:16
  113.2 10.3 %collective-permute-start.6 = (bf16[32,8,128]{2,1,0:T(8,128)(2,1)S(1)}, bf16[32,8,128]{2,1,0:T(8,128)(2,1)S(1)}, u32[]{:S(2)}, u32[]{:S(2)}) collective-permute-start(bf16[32,8,128]{2,1,0:T(8,128)(2,1)S(1)} %fusion.295), channel_id=1, source_target_pairs={{4,0},{8,4},{12,8},{5,1},{9,5},{13,9},{6,2},{10,6},{14,10},{7,3},{... | collective-permute-start | bytes 196616 | tf_op jit(solution)/shard_map/while/body/eval_jaxpr/ppermute | solution.py:17
  114.5 9.1 %collective-permute-start.7 = (bf16[32,8,128]{2,1,0:T(8,128)(2,1)S(1)}, bf16[32,8,128]{2,1,0:T(8,128)(2,1)S(1)}, u32[]{:S(2)}, u32[]{:S(2)}) collective-permute-start(bf16[32,8,128]{2,1,0:T(8,128)(2,1)S(1)} %fusion.295), channel_id=1, source_target_pairs={{0,4},{4,8},{8,12},{1,5},{5,9},{9,13},{2,6},{6,10},{10,14},{3,7},{... | collective-permute-start | bytes 196616 | tf_op jit(solution)/shard_map/while/body/eval_jaxpr/ppermute | solution.py:16
  123.9 5.1 %collective-permute-start.9 = (bf16[32,8,128]{2,1,0:T(8,128)(2,1)S(1)}, bf16[32,8,128]{2,1,0:T(8,128)(2,1)S(1)}, u32[]{:S(2)}, u32[]{:S(2)}) collective-permute-start(bf16[32,8,128]{2,1,0:T(8,128)(2,1)S(1)} %get-tuple-element.726), channel_id=1, source_target_pairs={} | collective-permute-start | bytes 196616 | tf_op jit(solution)/shard_map/while/body/eval_jaxpr/ppermute | solution.py:29
  124.6 6.2 %collective-permute-start.8 = (bf16[32,8,128]{2,1,0:T(8,128)(2,1)S(1)}, bf16[32,8,128]{2,1,0:T(8,128)(2,1)S(1)}, u32[]{:S(2)}, u32[]{:S(2)}) collective-permute-start(bf16[32,8,128]{2,1,0:T(8,128)(2,1)S(1)} %get-tuple-element.725), channel_id=1, source_target_pairs={{0,2},{1,3},{4,6},{5,7},{8,10},{9,11},{12,14},{13,15},{16,18},{17,... | collective-permute-start | bytes 196616 | tf_op jit(solution)/shard_map/while/body/eval_jaxpr/ppermute | solution.py:29
  137.5 7.0 %collective-permute-start = (bf16[192,1,128]{2,1,0:T(2,128)(2,1)S(1)}, bf16[192,1,128]{2,1,0:T(2,128)(2,1)S(1)}, u32[]{:S(2)}, u32[]{:S(2)}) collective-permute-start(bf16[192,1,128]{2,1,0:T(2,128)(2,1)S(1)} %get-tuple-element.689), channel_id=1, source_target_pairs={{4,0},{8,4},{12,8},{5,1},{9,5},{13,9},{6,2},{10,6},{14,10},{7,3},{... | collective-permute-start | bytes 147464 | tf_op jit(solution)/shard_map/while/body/eval_jaxpr/ppermute | solution.py:17
  138.8 6.9 %collective-permute-start.1 = (bf16[192,1,128]{2,1,0:T(2,128)(2,1)S(1)}, bf16[192,1,128]{2,1,0:T(2,128)(2,1)S(1)}, u32[]{:S(2)}, u32[]{:S(2)}) collective-permute-start(bf16[192,1,128]{2,1,0:T(2,128)(2,1)S(1)} %get-tuple-element.690), channel_id=1, source_target_pairs={{0,4},{4,8},{8,12},{1,5},{5,9},{9,13},{2,6},{6,10},{10,14},{3,7},{... | collective-permute-start | bytes 147464 | tf_op jit(solution)/shard_map/while/body/eval_jaxpr/ppermute | solution.py:16
  154.9 6.3 %collective-permute-start.2 = (bf16[64,1,128]{2,1,0:T(2,128)(2,1)S(1)}, bf16[64,1,128]{2,1,0:T(2,128)(2,1)S(1)}, u32[]{:S(2)}, u32[]{:S(2)}) collective-permute-start(bf16[64,1,128]{2,1,0:T(2,128)(2,1)S(1)} %get-tuple-element.699), channel_id=1, source_target_pairs={{4,0},{8,4},{12,8},{5,1},{9,5},{13,9},{6,2},{10,6},{14,10},{7,3},{... | collective-permute-start | bytes 49160 | tf_op jit(solution)/shard_map/while/body/eval_jaxpr/ppermute | solution.py:17
  156.2 6.6 %collective-permute-start.3 = (bf16[64,1,128]{2,1,0:T(2,128)(2,1)S(1)}, bf16[64,1,128]{2,1,0:T(2,128)(2,1)S(1)}, u32[]{:S(2)}, u32[]{:S(2)}) collective-permute-start(bf16[64,1,128]{2,1,0:T(2,128)(2,1)S(1)} %get-tuple-element.700), channel_id=1, source_target_pairs={{0,4},{4,8},{8,12},{1,5},{5,9},{9,13},{2,6},{6,10},{10,14},{3,7},{... | collective-permute-start | bytes 49160 | tf_op jit(solution)/shard_map/while/body/eval_jaxpr/ppermute | solution.py:16
  167.2 7.9 %collective-permute-start.4 = (bf16[64,1,128]{2,1,0:T(2,128)(2,1)S(1)}, bf16[64,1,128]{2,1,0:T(2,128)(2,1)S(1)}, u32[]{:S(2)}, u32[]{:S(2)}) collective-permute-start(bf16[64,1,128]{2,1,0:T(2,128)(2,1)S(1)} %get-tuple-element.709), channel_id=1, source_target_pairs={{4,0},{8,4},{12,8},{5,1},{9,5},{13,9},{6,2},{10,6},{14,10},{7,3},{... | collective-permute-start | bytes 49160 | tf_op jit(solution)/shard_map/while/body/eval_jaxpr/ppermute | solution.py:17
  168.5 6.6 %collective-permute-start.5 = (bf16[64,1,128]{2,1,0:T(2,128)(2,1)S(1)}, bf16[64,1,128]{2,1,0:T(2,128)(2,1)S(1)}, u32[]{:S(2)}, u32[]{:S(2)}) collective-permute-start(bf16[64,1,128]{2,1,0:T(2,128)(2,1)S(1)} %get-tuple-element.710), channel_id=1, source_target_pairs={{0,4},{4,8},{8,12},{1,5},{5,9},{9,13},{2,6},{6,10},{10,14},{3,7},{... | collective-permute-start | bytes 49160 | tf_op jit(solution)/shard_map/while/body/eval_jaxpr/ppermute | solution.py:16
  177.6 10.3 %collective-permute-start.6 = (bf16[32,8,128]{2,1,0:T(8,128)(2,1)S(1)}, bf16[32,8,128]{2,1,0:T(8,128)(2,1)S(1)}, u32[]{:S(2)}, u32[]{:S(2)}) collective-permute-start(bf16[32,8,128]{2,1,0:T(8,128)(2,1)S(1)} %fusion.295), channel_id=1, source_target_pairs={{4,0},{8,4},{12,8},{5,1},{9,5},{13,9},{6,2},{10,6},{14,10},{7,3},{... | collective-permute-start | bytes 196616 | tf_op jit(solution)/shard_map/while/body/eval_jaxpr/ppermute | solution.py:17
  178.9 9.1 %collective-permute-start.7 = (bf16[32,8,128]{2,1,0:T(8,128)(2,1)S(1)}, bf16[32,8,128]{2,1,0:T(8,128)(2,1)S(1)}, u32[]{:S(2)}, u32[]{:S(2)}) collective-permute-start(bf16[32,8,128]{2,1,0:T(8,128)(2,1)S(1)} %fusion.295), channel_id=1, source_target_pairs={{0,4},{4,8},{8,12},{1,5},{5,9},{9,13},{2,6},{6,10},{10,14},{3,7},{... | collective-permute-start | bytes 196616 | tf_op jit(solution)/shard_map/while/body/eval_jaxpr/ppermute | solution.py:16
  189.0 6.2 %collective-permute-start.8 = (bf16[32,8,128]{2,1,0:T(8,128)(2,1)S(1)}, bf16[32,8,128]{2,1,0:T(8,128)(2,1)S(1)}, u32[]{:S(2)}, u32[]{:S(2)}) collective-permute-start(bf16[32,8,128]{2,1,0:T(8,128)(2,1)S(1)} %get-tuple-element.725), channel_id=1, source_target_pairs={{0,2},{1,3},{4,6},{5,7},{8,10},{9,11},{12,14},{13,15},{16,18},{17,... | collective-permute-start | bytes 196616 | tf_op jit(solution)/shard_map/while/body/eval_jaxpr/ppermute | solution.py:29
  201.8 7.0 %collective-permute-start = (bf16[192,1,128]{2,1,0:T(2,128)(2,1)S(1)}, bf16[192,1,128]{2,1,0:T(2,128)(2,1)S(1)}, u32[]{:S(2)}, u32[]{:S(2)}) collective-permute-start(bf16[192,1,128]{2,1,0:T(2,128)(2,1)S(1)} %get-tuple-element.689), channel_id=1, source_target_pairs={{4,0},{8,4},{12,8},{5,1},{9,5},{13,9},{6,2},{10,6},{14,10},{7,3},{... | collective-permute-start | bytes 147464 | tf_op jit(solution)/shard_map/while/body/eval_jaxpr/ppermute | solution.py:17
  203.1 6.9 %collective-permute-start.1 = (bf16[192,1,128]{2,1,0:T(2,128)(2,1)S(1)}, bf16[192,1,128]{2,1,0:T(2,128)(2,1)S(1)}, u32[]{:S(2)}, u32[]{:S(2)}) collective-permute-start(bf16[192,1,128]{2,1,0:T(2,128)(2,1)S(1)} %get-tuple-element.690), channel_id=1, source_target_pairs={{0,4},{4,8},{8,12},{1,5},{5,9},{9,13},{2,6},{6,10},{10,14},{3,7},{... | collective-permute-start | bytes 147464 | tf_op jit(solution)/shard_map/while/body/eval_jaxpr/ppermute | solution.py:16
  219.3 6.3 %collective-permute-start.2 = (bf16[64,1,128]{2,1,0:T(2,128)(2,1)S(1)}, bf16[64,1,128]{2,1,0:T(2,128)(2,1)S(1)}, u32[]{:S(2)}, u32[]{:S(2)}) collective-permute-start(bf16[64,1,128]{2,1,0:T(2,128)(2,1)S(1)} %get-tuple-element.699), channel_id=1, source_target_pairs={{4,0},{8,4},{12,8},{5,1},{9,5},{13,9},{6,2},{10,6},{14,10},{7,3},{... | collective-permute-start | bytes 49160 | tf_op jit(solution)/shard_map/while/body/eval_jaxpr/ppermute | solution.py:17
  220.6 6.6 %collective-permute-start.3 = (bf16[64,1,128]{2,1,0:T(2,128)(2,1)S(1)}, bf16[64,1,128]{2,1,0:T(2,128)(2,1)S(1)}, u32[]{:S(2)}, u32[]{:S(2)}) collective-permute-start(bf16[64,1,128]{2,1,0:T(2,128)(2,1)S(1)} %get-tuple-element.700), channel_id=1, source_target_pairs={{0,4},{4,8},{8,12},{1,5},{5,9},{9,13},{2,6},{6,10},{10,14},{3,7},{... | collective-permute-start | bytes 49160 | tf_op jit(solution)/shard_map/while/body/eval_jaxpr/ppermute | solution.py:16
  231.6 7.9 %collective-permute-start.4 = (bf16[64,1,128]{2,1,0:T(2,128)(2,1)S(1)}, bf16[64,1,128]{2,1,0:T(2,128)(2,1)S(1)}, u32[]{:S(2)}, u32[]{:S(2)}) collective-permute-start(bf16[64,1,128]{2,1,0:T(2,128)(2,1)S(1)} %get-tuple-element.709), channel_id=1, source_target_pairs={{4,0},{8,4},{12,8},{5,1},{9,5},{13,9},{6,2},{10,6},{14,10},{7,3},{... | collective-permute-start | bytes 49160 | tf_op jit(solution)/shard_map/while/body/eval_jaxpr/ppermute | solution.py:17
  232.9 6.6 %collective-permute-start.5 = (bf16[64,1,128]{2,1,0:T(2,128)(2,1)S(1)}, bf16[64,1,128]{2,1,0:T(2,128)(2,1)S(1)}, u32[]{:S(2)}, u32[]{:S(2)}) collective-permute-start(bf16[64,1,128]{2,1,0:T(2,128)(2,1)S(1)} %get-tuple-element.710), channel_id=1, source_target_pairs={{0,4},{4,8},{8,12},{1,5},{5,9},{9,13},{2,6},{6,10},{10,14},{3,7},{... | collective-permute-start | bytes 49160 | tf_op jit(solution)/shard_map/while/body/eval_jaxpr/ppermute | solution.py:16
  242.0 10.3 %collective-permute-start.6 = (bf16[32,8,128]{2,1,0:T(8,128)(2,1)S(1)}, bf16[32,8,128]{2,1,0:T(8,128)(2,1)S(1)}, u32[]{:S(2)}, u32[]{:S(2)}) collective-permute-start(bf16[32,8,128]{2,1,0:T(8,128)(2,1)S(1)} %fusion.295), channel_id=1, source_target_pairs={{4,0},{8,4},{12,8},{5,1},{9,5},{13,9},{6,2},{10,6},{14,10},{7,3},{... | collective-permute-start | bytes 196616 | tf_op jit(solution)/shard_map/while/body/eval_jaxpr/ppermute | solution.py:17
  243.3 9.0 %collective-permute-start.7 = (bf16[32,8,128]{2,1,0:T(8,128)(2,1)S(1)}, bf16[32,8,128]{2,1,0:T(8,128)(2,1)S(1)}, u32[]{:S(2)}, u32[]{:S(2)}) collective-permute-start(bf16[32,8,128]{2,1,0:T(8,128)(2,1)S(1)} %fusion.295), channel_id=1, source_target_pairs={{0,4},{4,8},{8,12},{1,5},{5,9},{9,13},{2,6},{6,10},{10,14},{3,7},{... | collective-permute-start | bytes 196616 | tf_op jit(solution)/shard_map/while/body/eval_jaxpr/ppermute | solution.py:16
  252.7 5.1 %collective-permute-start.9 = (bf16[32,8,128]{2,1,0:T(8,128)(2,1)S(1)}, bf16[32,8,128]{2,1,0:T(8,128)(2,1)S(1)}, u32[]{:S(2)}, u32[]{:S(2)}) collective-permute-start(bf16[32,8,128]{2,1,0:T(8,128)(2,1)S(1)} %get-tuple-element.726), channel_id=1, source_target_pairs={} | collective-permute-start | bytes 196616 | tf_op jit(solution)/shard_map/while/body/eval_jaxpr/ppermute | solution.py:29
  253.4 6.2 %collective-permute-start.8 = (bf16[32,8,128]{2,1,0:T(8,128)(2,1)S(1)}, bf16[32,8,128]{2,1,0:T(8,128)(2,1)S(1)}, u32[]{:S(2)}, u32[]{:S(2)}) collective-permute-start(bf16[32,8,128]{2,1,0:T(8,128)(2,1)S(1)} %get-tuple-element.725), channel_id=1, source_target_pairs={{0,2},{1,3},{4,6},{5,7},{8,10},{9,11},{12,14},{13,15},{16,18},{17,... | collective-permute-start | bytes 196616 | tf_op jit(solution)/shard_map/while/body/eval_jaxpr/ppermute | solution.py:29
  266.2 7.0 %collective-permute-start = (bf16[192,1,128]{2,1,0:T(2,128)(2,1)S(1)}, bf16[192,1,128]{2,1,0:T(2,128)(2,1)S(1)}, u32[]{:S(2)}, u32[]{:S(2)}) collective-permute-start(bf16[192,1,128]{2,1,0:T(2,128)(2,1)S(1)} %get-tuple-element.689), channel_id=1, source_target_pairs={{4,0},{8,4},{12,8},{5,1},{9,5},{13,9},{6,2},{10,6},{14,10},{7,3},{... | collective-permute-start | bytes 147464 | tf_op jit(solution)/shard_map/while/body/eval_jaxpr/ppermute | solution.py:17
  267.5 6.9 %collective-permute-start.1 = (bf16[192,1,128]{2,1,0:T(2,128)(2,1)S(1)}, bf16[192,1,128]{2,1,0:T(2,128)(2,1)S(1)}, u32[]{:S(2)}, u32[]{:S(2)}) collective-permute-start(bf16[192,1,128]{2,1,0:T(2,128)(2,1)S(1)} %get-tuple-element.690), channel_id=1, source_target_pairs={{0,4},{4,8},{8,12},{1,5},{5,9},{9,13},{2,6},{6,10},{10,14},{3,7},{... | collective-permute-start | bytes 147464 | tf_op jit(solution)/shard_map/while/body/eval_jaxpr/ppermute | solution.py:16
  283.6 6.3 %collective-permute-start.2 = (bf16[64,1,128]{2,1,0:T(2,128)(2,1)S(1)}, bf16[64,1,128]{2,1,0:T(2,128)(2,1)S(1)}, u32[]{:S(2)}, u32[]{:S(2)}) collective-permute-start(bf16[64,1,128]{2,1,0:T(2,128)(2,1)S(1)} %get-tuple-element.699), channel_id=1, source_target_pairs={{4,0},{8,4},{12,8},{5,1},{9,5},{13,9},{6,2},{10,6},{14,10},{7,3},{... | collective-permute-start | bytes 49160 | tf_op jit(solution)/shard_map/while/body/eval_jaxpr/ppermute | solution.py:17
  284.9 6.6 %collective-permute-start.3 = (bf16[64,1,128]{2,1,0:T(2,128)(2,1)S(1)}, bf16[64,1,128]{2,1,0:T(2,128)(2,1)S(1)}, u32[]{:S(2)}, u32[]{:S(2)}) collective-permute-start(bf16[64,1,128]{2,1,0:T(2,128)(2,1)S(1)} %get-tuple-element.700), channel_id=1, source_target_pairs={{0,4},{4,8},{8,12},{1,5},{5,9},{9,13},{2,6},{6,10},{10,14},{3,7},{... | collective-permute-start | bytes 49160 | tf_op jit(solution)/shard_map/while/body/eval_jaxpr/ppermute | solution.py:16
  295.9 7.9 %collective-permute-start.4 = (bf16[64,1,128]{2,1,0:T(2,128)(2,1)S(1)}, bf16[64,1,128]{2,1,0:T(2,128)(2,1)S(1)}, u32[]{:S(2)}, u32[]{:S(2)}) collective-permute-start(bf16[64,1,128]{2,1,0:T(2,128)(2,1)S(1)} %get-tuple-element.709), channel_id=1, source_target_pairs={{4,0},{8,4},{12,8},{5,1},{9,5},{13,9},{6,2},{10,6},{14,10},{7,3},{... | collective-permute-start | bytes 49160 | tf_op jit(solution)/shard_map/while/body/eval_jaxpr/ppermute | solution.py:17
  297.2 6.6 %collective-permute-start.5 = (bf16[64,1,128]{2,1,0:T(2,128)(2,1)S(1)}, bf16[64,1,128]{2,1,0:T(2,128)(2,1)S(1)}, u32[]{:S(2)}, u32[]{:S(2)}) collective-permute-start(bf16[64,1,128]{2,1,0:T(2,128)(2,1)S(1)} %get-tuple-element.710), channel_id=1, source_target_pairs={{0,4},{4,8},{8,12},{1,5},{5,9},{9,13},{2,6},{6,10},{10,14},{3,7},{... | collective-permute-start | bytes 49160 | tf_op jit(solution)/shard_map/while/body/eval_jaxpr/ppermute | solution.py:16
  306.4 10.3 %collective-permute-start.6 = (bf16[32,8,128]{2,1,0:T(8,128)(2,1)S(1)}, bf16[32,8,128]{2,1,0:T(8,128)(2,1)S(1)}, u32[]{:S(2)}, u32[]{:S(2)}) collective-permute-start(bf16[32,8,128]{2,1,0:T(8,128)(2,1)S(1)} %fusion.295), channel_id=1, source_target_pairs={{4,0},{8,4},{12,8},{5,1},{9,5},{13,9},{6,2},{10,6},{14,10},{7,3},{... | collective-permute-start | bytes 196616 | tf_op jit(solution)/shard_map/while/body/eval_jaxpr/ppermute | solution.py:17
  307.7 9.1 %collective-permute-start.7 = (bf16[32,8,128]{2,1,0:T(8,128)(2,1)S(1)}, bf16[32,8,128]{2,1,0:T(8,128)(2,1)S(1)}, u32[]{:S(2)}, u32[]{:S(2)}) collective-permute-start(bf16[32,8,128]{2,1,0:T(8,128)(2,1)S(1)} %fusion.295), channel_id=1, source_target_pairs={{0,4},{4,8},{8,12},{1,5},{5,9},{9,13},{2,6},{6,10},{10,14},{3,7},{... | collective-permute-start | bytes 196616 | tf_op jit(solution)/shard_map/while/body/eval_jaxpr/ppermute | solution.py:16
  317.1 5.1 %collective-permute-start.9 = (bf16[32,8,128]{2,1,0:T(8,128)(2,1)S(1)}, bf16[32,8,128]{2,1,0:T(8,128)(2,1)S(1)}, u32[]{:S(2)}, u32[]{:S(2)}) collective-permute-start(bf16[32,8,128]{2,1,0:T(8,128)(2,1)S(1)} %get-tuple-element.726), channel_id=1, source_target_pairs={} | collective-permute-start | bytes 196616 | tf_op jit(solution)/shard_map/while/body/eval_jaxpr/ppermute | solution.py:29
  317.8 6.2 %collective-permute-start.8 = (bf16[32,8,128]{2,1,0:T(8,128)(2,1)S(1)}, bf16[32,8,128]{2,1,0:T(8,128)(2,1)S(1)}, u32[]{:S(2)}, u32[]{:S(2)}) collective-permute-start(bf16[32,8,128]{2,1,0:T(8,128)(2,1)S(1)} %get-tuple-element.725), channel_id=1, source_target_pairs={{0,2},{1,3},{4,6},{5,7},{8,10},{9,11},{12,14},{13,15},{16,18},{17,... | collective-permute-start | bytes 196616 | tf_op jit(solution)/shard_map/while/body/eval_jaxpr/ppermute | solution.py:29
  (33 other events, 138.2 us)
where the time goes:
time: 327 us; the launch traced here: 325 us
  starting transfers between devices  146 us (45%)
  blocking collectives  47.4 us (14%)
  other arithmetic  32.7 us (10%)
  waiting for transfers between devices  28.1 us (9%)
  loops' own time  26.9 us (8%)
  local copies, waits for them, and re-layouts  22.6 us (7%)
  matrix products  20.8 us (6%)
    ppermute x20, starting transfers between devices, padded_2(): before = lax.ppermute(last, axis, up)  96.2 us
    concatenate x35, other arithmetic, padded_2(): array = jnp.concatenate([before, array, after], axis=dim)  30 us
    another operation x1, loops' own time, shards(): lax.fori_loop(0, segments + owners - 1, advance, initial)  26.9 us
    ppermute x20, starting transfers between devices, padded_2(): after = lax.ppermute(first, axis, down)  25.8 us
    ppermute x10, starting transfers between devices, shifted(): return lax.ppermute(block, axis, route)  23.9 us
    dot_general x135, matrix products, convolve_rows(): jnp.dot(weights[tap_index], window, preferred_element_type=jnp.float32)  20.8 us
    all_gather x10, blocking collectives, block_conv(): whole_input = lax.all_gather(own_part, 'chan', axis=0, tiled=True)  19 us
    ppermute x20, waiting for transfers between devices, padded_2(): before = lax.ppermute(last, axis, up)  13.7 us
  transfers between devices with their start and end apart: 50, of which 20 were waited for; matrix products, arithmetic and copies ran while one was open for 2% of the time, Pallas kernels for 0%

commit v1 on v0

--- a/solution.py
+++ b/solution.py
@@ -1,6 +1,10 @@
+import functools
+
 import jax
 import jax.numpy as jnp
 from jax import lax
+from jax.experimental import pallas as pl
+from jax.experimental.pallas import tpu as pltpu
 from jax.sharding import PartitionSpec as P
 
 BH = 8
@@ -115,6 +119,320 @@
     return results
 
 
+MESH = pl.DeviceIdType.MESH
+
+
+def plain_kernel(
+    sizes,
+    lr_ref, fl_ref, wj_ref, w1_ref, w2_ref, bias_ref,
+    out_ref,
+    L, H, blank, FL, FS, WJ, W1, W2, B,
+    lr_send, lr_recv, fl_send, fl_recv, fl_sem, w_send, w_recv, h_send, h_recv, o_send, o_recv,
+):
+    frames, chans, tiles, rows, half, cols, blocks = sizes
+    halo = 1 + 2 * blocks
+    reach = rows + halo
+    full = half * chans
+    clip = lax.axis_index("clips")
+    z = lax.axis_index("tiles")
+    x = lax.axis_index("frames")
+    c = lax.axis_index("chan")
+    shot = x * chans + c
+    group = [(f, k) for f in range(frames) for k in range(chans)]
+
+    def has(step):
+        return (z + step >= 0) & (z + step < tiles)
+
+    def not_me(f, k):
+        return jnp.logical_not((x == f) & (c == k))
+
+    def half_of(k):
+        return pl.ds(k * half if isinstance(k, int) else pl.multiple_of(k * half, half), half)
+
+    def remote(src, dst, send, recv, dev):
+        return pltpu.make_async_remote_copy(
+            src_ref=src, dst_ref=dst, send_sem=send, recv_sem=recv,
+            device_id=(clip,) + dev, device_id_type=MESH,
+        )
+
+    for f in range(frames):
+        for part in (slice(0, halo), slice(halo + rows, 2 * halo + rows)):
+            L[f, part] = jnp.zeros((halo, full, cols), L.dtype)
+        for part in (slice(0, reach), slice(reach + rows, 2 * reach + rows)):
+            H[f, part] = jnp.zeros((reach, full, cols), H.dtype)
+    FL[...] = jnp.zeros(FL.shape, FL.dtype)
+
+    barrier = pltpu.get_barrier_semaphore()
+
+    def greet(dev):
+        pl.semaphore_signal(barrier, inc=1, device_id=(clip,) + dev, device_id_type=MESH)
+
+    count = len(group) - 1
+    for f, k in group:
+        @pl.when(not_me(f, k))
+        def _():
+            greet((z, f, k))
+    for step in (-1, 1):
+        for f, k in group:
+            @pl.when(has(step))
+            def _():
+                greet((z + step, f, k))
+        count = count + jnp.where(has(step), len(group), 0)
+    for step in (-2, 2):
+        @pl.when(has(step))
+        def _():
+            greet((z + step, x, c))
+        count = count + jnp.where(has(step), 1, 0)
+    pl.semaphore_wait(barrier, count)
+
+    span = {0: (0, rows, halo), 1: (rows - halo, halo, 0), -1: (0, halo, halo + rows)}
+
+    def lr_copy(f, k, step, src_f, src_k):
+        start, length, land = span[step]
+        return remote(
+            lr_ref.at[f * chans + k, pl.ds(start, length)],
+            L.at[src_f, pl.ds(land, length), half_of(src_k)],
+            lr_send.at[f, k, step + 1], lr_recv.at[src_f, src_k, step + 1],
+            (z + step, f, k),
+        )
+
+    def w_copies(k, src_k):
+        pairs = [(wj_ref, WJ.at[:, half_of(src_k)]), (w1_ref, W1.at[:, :, half_of(src_k)]),
+                 (w2_ref, W2.at[:, :, half_of(src_k)]), (bias_ref, B.at[:, half_of(src_k)])]
+        return [remote(a, b, w_send.at[k, n], w_recv.at[src_k, n], (z, x, k))
+                for n, (a, b) in enumerate(pairs)]
+
+    def fl_copy(step):
+        return remote(fl_ref.at[shot], FL.at[1 - step], fl_send.at[step + 1],
+                      fl_recv.at[step + 1], (z + step, x, c))
+
+    for step in (0, -1, 1):
+        for f, k in group:
+            @pl.when(not_me(f, k) if step == 0 else has(step))
+            def _():
+                lr_copy(f, k, step, x, c).start()
+    for k in range(chans):
+        @pl.when(c != k)
+        def _():
+            for copy in w_copies(k, c):
+                copy.start()
+    for step in (-1, 1):
+        @pl.when(has(step))
+        def _():
+            fl_copy(step).start()
+    L[x, halo:halo + rows, half_of(c), :] = lr_ref[shot]
+    WJ[:, half_of(c), :] = wj_ref[...]
+    W1[:, :, half_of(c), :] = w1_ref[...]
+    W2[:, :, half_of(c), :] = w2_ref[...]
+    B[:, half_of(c), :] = bias_ref[...]
+    FL[1] = fl_ref[shot]
+    blank[...] = jnp.zeros(blank.shape, blank.dtype)
+    for step in (-1, 1):
+        @pl.when(has(-step))
+        def _():
+            fl_copy(step).wait_recv()
+    to_scalars = pltpu.make_async_copy(FL, FS, fl_sem)
+    to_scalars.start()
+    to_scalars.wait()
+
+    lane = lax.broadcasted_iota(jnp.int32, (full, cols), 1)
+
+    def displaced(which, t):
+        age = t - 1 - which
+        rows_out = []
+        for j in range(-halo, rows + halo):
+            near = 0 if j < 0 else (1 if j < rows else 2)
+            entry = (which * frames + t) * 2
+            dy = FS[near, entry, 0]
+            dx = FS[near, entry + 1, 0]
+            source = reach + j + dy
+            v = (H[age, source] if age >= 0 else blank[source]).astype(jnp.float32)
+            turned = pltpu.roll(v, lax.rem(cols - dx, cols), 1)
+            seen = lane + dx
+            rows_out.append(
+                jnp.where((seen >= 0) & (seen < cols), turned, 0.0).astype(jnp.bfloat16))
+        return jnp.concatenate(rows_out, axis=1)
+
+    def conv(weights, inputs, count, bias):
+        y = jnp.dot(weights, inputs, preferred_element_type=jnp.float32)
+        result = []
+        for r in range(1, count - 1):
+            sides = []
+            for j in range(3):
+                total = None
+                for i in range(3):
+                    first = (3 * i + j) * full
+                    part = y[first:first + full, (r + i - 1) * cols:(r + i) * cols]
+                    total = part if total is None else total + part
+                sides.append(total)
+            left = jnp.where(lane == 0, 0.0, pltpu.roll(sides[0], 1, 1))
+            right = jnp.where(lane == cols - 1, 0.0, pltpu.roll(sides[2], cols - 1, 1))
+            result.append(sides[1] + left + right + bias)
+        return result
+
+    def inside(values, first):
+        kept = []
+        for n, v in enumerate(values):
+            j = first + n
+            if j < 0:
+                v = jnp.where(z > 0, v, 0.0)
+            elif j >= rows:
+                v = jnp.where(z < tiles - 1, v, 0.0)
+            kept.append(v.astype(jnp.bfloat16))
+        return kept
+
+    def h_copy(t, step):
+        start, length = (0, rows) if abs(step) == 1 else ((rows - halo, halo) if step > 0 else (0, halo))
+        return remote(
+            H.at[t, pl.ds(reach + start, length)],
+            H.at[t, pl.ds(reach + start - step * rows, length)],
+            h_send.at[t, step + 2], h_recv.at[t, step + 2], (z + step, x, c),
+        )
+
+    def o_copy(t, k, to_shot, src):
+        return remote(H.at[t, pl.ds(reach, rows), half_of(k)], out_ref.at[to_shot],
+                      o_send.at[t, k], o_recv.at[src], (z, t, k))
+
+    for t in range(frames):
+        warped_two = displaced(1, t)
+        if t == 0:
+            warped_one = displaced(0, t)
+            for k in range(chans):
+                @pl.when(c != k)
+                def _():
+                    for copy in w_copies(c, k):
+                        copy.wait_recv()
+        for k in range(chans):
+            @pl.when(not_me(t, k))
+            def _():
+                lr_copy(x, c, 0, t, k).wait_recv()
+            for step in (-1, 1):
+                @pl.when(has(-step))
+                def _():
+                    lr_copy(x, c, step, t, k).wait_recv()
+        if t > 0:
+            for step in (-2, -1, 1, 2):
+                @pl.when(has(-step))
+                def _():
+                    h_copy(t - 1, step).wait_recv()
+            warped_one = displaced(0, t)
+        current = jnp.concatenate([L[t, r] for r in range(rows + 2 * halo)], axis=1)
+        stacked = jnp.concatenate([current, warped_one, warped_two], axis=0)
+        edge = halo - 1
+        joined = conv(WJ[...].reshape(9 * full, 3 * full), stacked, rows + 2 * halo, B[0])
+        state = inside([jnp.maximum(v, 0.1 * v) for v in joined], -edge)
+        for n in range(blocks):
+            inner = conv(W1[n].reshape(9 * full, full), jnp.concatenate(state, axis=1),
+                         rows + 2 * edge, B[1 + n])
+            inner = inside([jnp.maximum(v, 0.0) for v in inner], 1 - edge)
+            added = conv(W2[n].reshape(9 * full, full), jnp.concatenate(inner, axis=1),
+                         rows + 2 * edge - 2, B[1 + blocks + n])
+            state = inside([s.astype(jnp.float32) + v for s, v in zip(state[2:-2], added)],
+                           2 - edge)
+            edge -= 2
+        for r in range(rows):
+            H[t, reach + r] = state[r]
+        if t < frames - 1:
+            for step in (-1, 1, -2, 2):
+                @pl.when(has(step))
+                def _():
+                    h_copy(t, step).start()
+        for k in range(chans):
+            @pl.when(not_me(t, k))
+            def _():
+                o_copy(t, k, shot, shot).start()
+
+            @pl.when((x == t) & (c == k))
+            def _():
+                out_ref[shot] = H[t, reach:reach + rows, half_of(k), :]
+
+    for f, k in group:
+        @pl.when(not_me(f, k))
+        def _():
+            lr_copy(f, k, 0, x, c).wait_send()
+            o_copy(0, 0, f * chans + k, f * chans + k).wait_recv()
+        for step in (-1, 1):
+            @pl.when(has(step))
+            def _():
+                lr_copy(f, k, step, x, c).wait_send()
+    for k in range(chans):
+        @pl.when(c != k)
+        def _():
+            for copy in w_copies(k, c):
+                copy.wait_send()
+    for step in (-1, 1):
+        @pl.when(has(step))
+        def _():
+            fl_copy(step).wait_send()
+    for t in range(frames):
+        if t < frames - 1:
+            for step in (-1, 1, -2, 2):
+                @pl.when(has(step))
+                def _():
+                    h_copy(t, step).wait_send()
+        for k in range(chans):
+            @pl.when(not_me(t, k))
+            def _():
+                o_copy(t, k, shot, shot).wait_send()
+
+
+def by_shots(lr_feats, flow_prev, flow_second, w_join, b_join, w_first, b_first, w_second, b_second):
+    shots, _, half, rows, cols = lr_feats.shape
+    frames = lax.axis_size("frames")
+    chans = lax.axis_size("chan")
+    tiles = lax.axis_size("tiles")
+    blocks = w_first.shape[0]
+    halo = 1 + 2 * blocks
+    reach = rows + halo
+    full = half * chans
+    lr = jnp.swapaxes(lr_feats[:, 0], 1, 2)
+    flows = jnp.stack([flow_prev[:, :, 0], flow_second[:, :, 0]], axis=1).reshape(shots, 4 * frames)
+    flows = jnp.broadcast_to(flows[:, :, None], (shots, 4 * frames, 128))
+    bias = jnp.concatenate([b_join[None], b_first, b_second], axis=0)
+    bias = jnp.broadcast_to(bias[:, :, None], bias.shape + (cols,))
+    kind = lr.dtype
+    dma = pltpu.SemaphoreType.DMA
+    out = pl.pallas_call(
+        functools.partial(plain_kernel, (frames, chans, tiles, rows, half, cols, blocks)),
+        out_shape=jax.ShapeDtypeStruct((shots, rows, half, cols), kind),
+        in_specs=[pl.BlockSpec(memory_space=pltpu.VMEM)] * 6,
+        out_specs=pl.BlockSpec(memory_space=pltpu.VMEM),
+        scratch_shapes=[
+            pltpu.VMEM((frames, rows + 2 * halo, full, cols), kind),
+            pltpu.VMEM((frames, rows + 2 * reach, full, cols), kind),
+            pltpu.VMEM((rows + 2 * reach, full, cols), kind),
+            pltpu.VMEM((3, 4 * frames, 128), jnp.int32),
+            pltpu.SMEM((3, 4 * frames, 128), jnp.int32),
+            pltpu.VMEM((9, full, 3 * full), kind),
+            pltpu.VMEM((blocks, 9, full, full), kind),
+            pltpu.VMEM((blocks, 9, full, full), kind),
+            pltpu.VMEM((1 + 2 * blocks, full, cols), jnp.float32),
+            dma((frames, chans, 3)), dma((frames, chans, 3)), dma((3,)), dma((3,)), dma,
+            dma((chans, 4)), dma((chans, 4)), dma((frames, 5)), dma((frames, 5)),
+            dma((frames, chans)), dma((shots,)),
+        ],
+        compiler_params=pltpu.CompilerParams(
+            collective_id=0, has_side_effects=True, vmem_limit_bytes=40 * 1024 * 1024
+        ),
+    )(lr, flows, w_join, w_first, w_second, bias)
+    return jnp.swapaxes(out, 1, 2)[:, None]
+
+
+def one_shot_each(lr_feats, flow_prev, flow_second, w_join, b_join, w_first, *rest):
+    halo = 1 + 2 * w_first.shape[0]
+    rows = lr_feats.shape[3]
+    shots = lax.axis_size("frames") * lax.axis_size("chan")
+    fits = (
+        lr_feats.shape[0] == shots
+        and flow_prev.shape[1] == lax.axis_size("frames")
+        and flow_prev.shape[2] == 1
+        and halo <= rows
+        and lr_feats.shape[4] == 128
+    )
+    plan = by_shots if fits else shards
+    return plan(lr_feats, flow_prev, flow_second, w_join, b_join, w_first, *rest)
+
+
 def solution(mesh):
     in_specs = (
         P("clips", "frames", "chan", "tiles", None),
@@ -128,4 +446,4 @@
         P(None, "chan"),
     )
     out_specs = P("clips", "frames", "chan", "tiles", None)
-    return jax.shard_map(shards, mesh=mesh, in_specs=in_specs, out_specs=out_specs, check_vma=False)
+    return jax.shard_map(one_shot_each, mesh=mesh, in_specs=in_specs, out_specs=out_specs, check_vma=False)

time: 327 us -> 27 us (0.08)
  starting transfers between devices: 146 us -> 0 us
  blocking collectives: 47.4 us -> 0 us
  other arithmetic: 32.7 us -> 0.01 us
  waiting for transfers between devices: 28.1 us -> 0 us
  loops' own time: 26.9 us -> 0 us
  Pallas kernels: 0 us -> 23.3 us
  matrix products: 20.8 us -> 0 us
  local copies, waits for them, and re-layouts: 22.6 us -> 3.44 us
    ppermute x50 -> x0, starting transfers between devices: 146 us -> none  [the longest x20 96.2 us: padded_2(): before = lax.ppermute(last, axis, up)]
    all_gather x25 -> x0, blocking collectives: 47.4 us -> none  [the longest x10 19 us: block_conv(): whole_input = lax.all_gather(own_part, 'chan', axis=0, tiled=True)]
    concatenate x40 -> x1, other arithmetic: 30.2 us -> 0.01 us  [by_shots(): bias = jnp.concatenate([b_join[None], b_first, b_second], axis=0)]
    ppermute x50 -> x0, waiting for transfers between devices: 28.1 us -> none  [the longest x20 13.7 us: padded_2(): before = lax.ppermute(last, axis, up)]
    another operation x1 -> x0, loops' own time: 26.9 us -> none  [shards(): lax.fori_loop(0, segments + owners - 1, advance, initial)]
    pallas_call x0 -> x1, Pallas kernels: none -> 23.3 us  [by_shots(): pl.pallas_call(functools.partial(plain_kernel, (frames, chans, tiles, row...]
    dot_general x135 -> x0, matrix products: 20.8 us -> none  [convolve_rows(): jnp.dot(weights[tap_index], window, preferred_element_type=jnp.float32)]
    slice x40 -> x0, local copies, waits for them, and re-layouts: 14.2 us -> none  [the longest x15 6.92 us: convolve_rows(): padded[:, tap_row:tap_row + row_count, tap_col:tap_col + col_count]]
  transfers between devices with their start and end apart: 50 -> 0, of which waited for: 20 -> 0; matrix products, arithmetic and copies ran while one was open for 2% -> 0% of each run, Pallas kernels for 0% -> 0%
where the time goes in v1:
time: 27 us; the launch traced here: 26.8 us
  Pallas kernels  23.3 us (86%)
  local copies, waits for them, and re-layouts  3.44 us (13%)
    pallas_call x1, Pallas kernels, by_shots(): pl.pallas_call(functools.partial(plain_kernel, (frames, chans, tiles, row...  23.3 us
    unnamed x17, local copies, waits for them, and re-layouts  2.4 us
    broadcast_in_dim x1, local copies, waits for them, and re-layouts, by_shots(): return jnp.swapaxes(out, 1, 2)[:, None]  0.81 us

profile of v1, /device:TPU:0, one launch (start us, length us, event | category | flops | bytes accessed | tf_op | source)
XLA Modules:
  0.0 26.8 jit_solution(16365468255850837311)
XLA Ops:
  0.0 0.0 copy-start.5
  0.0 0.0 copy-start.6
  0.0 0.0 copy-start.7
  0.0 0.0 copy-start.4
  0.0 0.6 %copy-done.5 = f32[1,32]{1,0:T(1,128)S(1)} copy-done((f32[1,32]{1,0:T(1,128)S(1)}, f32[1,32]{1,0:T(1,128)}, u32[]{:S(2)}) %copy-start.5) | copy-done | bytes 152
  0.7 0.0 copy-done.6
  0.7 0.0 copy-done.7
  0.7 0.0 copy-start.3
  0.7 0.0 copy-done.4
  0.7 0.6 %copy-done.3 = s32[4,2,1,2]{0,3,2,1:T(2,128)S(1)} copy-done((s32[4,2,1,2]{0,3,2,1:T(2,128)S(1)}, s32[4,2,1,2]{0,3,2,1:T(2,128)}, u32[]{:S(2)}) %copy-start.3) | copy-done | bytes 88
  1.4 0.1 copy.11
  1.5 0.1 broadcast_in_dim.20.fl_ref
  1.5 0.1 broadcast_in_dim.22.bias_ref
  1.6 0.0 copy-start
  1.6 0.0 copy-start.1
  1.6 0.0 copy-start.2
  1.6 1.0 %copy.14 = bf16[4,1,32,8,128]{4,2,3,0,1:T(8,128)(2,1)S(1)} copy(bf16[4,1,32,8,128]{4,3,2,1,0:T(8,128)(2,1)} %param.9) | data formatting | bytes 524288 | tf_op args[0]
  2.7 0.0 copy-done
  2.7 0.0 copy-done.1
  2.7 0.0 copy-done.2
  2.7 23.3 %shard_map.91 = bf16[4,8,32,128]{3,2,1,0:T(8,128)(2,1)S(1)} custom-call(bf16[4,8,32,128]{3,2,1,0:T(8,128)(2,1)S(1)} %bitcast.13, s32[4,8,128]{2,1,0:T(8,128)S(1)} %broadcast_in_dim.20.fl_ref, bf16[9,32,192]{2,1,0:T(8,128)(2,1)S(1)} %copy-done, bf16[1,9,32,64]{3,2,1,0:T(8,128)(2,1)S(1)} %copy-done.1, bf16[1,9,32,64]{3,2,1,0:T(8,128)(2,1)S(1)} %copy-done.2, ...), custom_call_target="tpu_custom_call" | custom-call | tf_op jit(solution)/shard_map/pallas_call | solution.py:395
  26.0 0.8 %copy.12 = bf16[4,1,32,8,128]{4,3,2,1,0:T(8,128)(2,1)} copy(bf16[4,1,32,8,128]{4,2,3,0,1:T(8,128)(2,1)S(1)} %bitcast.12) | data formatting | bytes 524288 | tf_op jit(solution)/shard_map/broadcast_in_dim | solution.py:418
  (2 shorter events, 0.0 us)
Async XLA Ops:
  0.0 0.7 %copy-start.5 = (f32[1,32]{1,0:T(1,128)S(1)}, f32[1,32]{1,0:T(1,128)}, u32[]{:S(2)}) copy-start(f32[1,32]{1,0:T(1,128)} %param.17) | copy-start | bytes 388
  0.0 0.7 %copy-start.6 = (f32[1,32]{1,0:T(1,128)S(1)}, f32[1,32]{1,0:T(1,128)}, u32[]{:S(2)}) copy-start(f32[1,32]{1,0:T(1,128)} %param.15) | copy-start | bytes 388
  0.0 0.7 %copy-start.7 = (f32[32]{0:T(128)S(1)}, f32[32]{0:T(128)}, u32[]{:S(2)}) copy-start(f32[32]{0:T(128)} %param.13) | copy-start | bytes 388
  0.0 0.7 %copy-start.4 = (s32[4,2,1,2]{0,3,2,1:T(2,128)S(1)}, s32[4,2,1,2]{0,3,2,1:T(2,128)}, u32[]{:S(2)}) copy-start(s32[4,2,1,2]{0,3,2,1:T(2,128)} %param.10) | copy-start | bytes 196
  0.7 0.7 %copy-start.3 = (s32[4,2,1,2]{0,3,2,1:T(2,128)S(1)}, s32[4,2,1,2]{0,3,2,1:T(2,128)}, u32[]{:S(2)}) copy-start(s32[4,2,1,2]{0,3,2,1:T(2,128)} %param.11) | copy-start | bytes 196
  1.6 1.1 %copy-start = (bf16[9,32,192]{2,1,0:T(8,128)(2,1)S(1)}, bf16[9,32,192]{2,1,0:T(8,128)(2,1)}, u32[]{:S(2)}) copy-start(bf16[9,32,192]{2,1,0:T(8,128)(2,1)} %wj_ref.1) | copy-start | bytes 331780
  1.6 1.1 %copy-start.1 = (bf16[1,9,32,64]{3,2,1,0:T(8,128)(2,1)S(1)}, bf16[1,9,32,64]{3,2,1,0:T(8,128)(2,1)}, u32[]{:S(2)}) copy-start(bf16[1,9,32,64]{3,2,1,0:T(8,128)(2,1)} %w1_ref.1) | copy-start | bytes 110596
  1.6 1.1 %copy-start.2 = (bf16[1,9,32,64]{3,2,1,0:T(8,128)(2,1)S(1)}, bf16[1,9,32,64]{3,2,1,0:T(8,128)(2,1)}, u32[]{:S(2)}) copy-start(bf16[1,9,32,64]{3,2,1,0:T(8,128)(2,1)} %w2_ref.1) | copy-start | bytes 110596

commit v2 on v1

--- a/solution.py
+++ b/solution.py
@@ -124,9 +124,9 @@
 
 def plain_kernel(
     sizes,
-    lr_ref, fl_ref, wj_ref, w1_ref, w2_ref, bias_ref,
+    lr_ref, fp_ref, fs_ref, wj_ref, w1_ref, w2_ref, bj_ref, b1_ref, b2_ref,
     out_ref,
-    L, H, blank, FL, FS, WJ, W1, W2, B,
+    L, H, blank, FA, FL, FS, WJ, W1, W2, BA, B,
     lr_send, lr_recv, fl_send, fl_recv, fl_sem, w_send, w_recv, h_send, h_recv, o_send, o_recv,
 ):
     frames, chans, tiles, rows, half, cols, blocks = sizes
@@ -161,6 +161,12 @@
         for part in (slice(0, reach), slice(reach + rows, 2 * reach + rows)):
             H[f, part] = jnp.zeros((reach, full, cols), H.dtype)
     FL[...] = jnp.zeros(FL.shape, FL.dtype)
+    FA[...] = jnp.zeros(FA.shape, FA.dtype)
+    BA[...] = jnp.zeros(BA.shape, BA.dtype)
+    FA[0, :, 0:frames * chans] = fp_ref[...]
+    FA[1, :, 0:frames * chans] = fs_ref[...]
+    for n, ref in enumerate([bj_ref] + [b1_ref.at[m:m + 1] for m in range(blocks)] + [b2_ref.at[m:m + 1] for m in range(blocks)]):
+        BA[n:n + 1, 0:half] = ref[...]
 
     barrier = pltpu.get_barrier_semaphore()
 
@@ -198,34 +204,40 @@
 
     def w_copies(k, src_k):
         pairs = [(wj_ref, WJ.at[:, half_of(src_k)]), (w1_ref, W1.at[:, :, half_of(src_k)]),
-                 (w2_ref, W2.at[:, :, half_of(src_k)]), (bias_ref, B.at[:, half_of(src_k)])]
+                 (w2_ref, W2.at[:, :, half_of(src_k)]), (BA, B.at[src_k])]
         return [remote(a, b, w_send.at[k, n], w_recv.at[src_k, n], (z, x, k))
                 for n, (a, b) in enumerate(pairs)]
 
     def fl_copy(step):
-        return remote(fl_ref.at[shot], FL.at[1 - step], fl_send.at[step + 1],
+        return remote(FA, FL.at[1 - step], fl_send.at[step + 1],
                       fl_recv.at[step + 1], (z + step, x, c))
 
-    for step in (0, -1, 1):
-        for f, k in group:
-            @pl.when(not_me(f, k) if step == 0 else has(step))
-            def _():
-                lr_copy(f, k, step, x, c).start()
-    for k in range(chans):
-        @pl.when(c != k)
-        def _():
-            for copy in w_copies(k, c):
-                copy.start()
+    def send_lr(f, k, step):
+        @pl.when(not_me(f, k) if step == 0 else has(step))
+        def _():
+            lr_copy(f, k, step, x, c).start()
+
     for step in (-1, 1):
         @pl.when(has(step))
         def _():
             fl_copy(step).start()
+    for turn in range(frames):
+        f = lax.rem(x + turn, frames)
+        for step in (0, -1, 1):
+            for k in range(chans):
+                send_lr(f, k, step)
+        if turn == 0:
+            for k in range(chans):
+                @pl.when(c != k)
+                def _():
+                    for copy in w_copies(k, c):
+                        copy.start()
     L[x, halo:halo + rows, half_of(c), :] = lr_ref[shot]
     WJ[:, half_of(c), :] = wj_ref[...]
     W1[:, :, half_of(c), :] = w1_ref[...]
     W2[:, :, half_of(c), :] = w2_ref[...]
-    B[:, half_of(c), :] = bias_ref[...]
-    FL[1] = fl_ref[shot]
+    B[c] = BA[...]
+    FL[1] = FA[...]
     blank[...] = jnp.zeros(blank.shape, blank.dtype)
     for step in (-1, 1):
         @pl.when(has(-step))
@@ -242,9 +254,8 @@
         rows_out = []
         for j in range(-halo, rows + halo):
             near = 0 if j < 0 else (1 if j < rows else 2)
-            entry = (which * frames + t) * 2
-            dy = FS[near, entry, 0]
-            dx = FS[near, entry + 1, 0]
+            dy = FS[near, which, 2 * t, shot]
+            dx = FS[near, which, 2 * t + 1, shot]
             source = reach + j + dy
             v = (H[age, source] if age >= 0 else blank[source]).astype(jnp.float32)
             turned = pltpu.roll(v, lax.rem(cols - dx, cols), 1)
@@ -293,6 +304,14 @@
         return remote(H.at[t, pl.ds(reach, rows), half_of(k)], out_ref.at[to_shot],
                       o_send.at[t, k], o_recv.at[src], (z, t, k))
 
+    corner = lax.broadcasted_iota(jnp.int32, (half, 128), 0) == lax.broadcasted_iota(
+        jnp.int32, (half, 128), 1)
+
+    def bias_of(n):
+        parts = [jnp.sum(jnp.where(corner, B[k, n:n + 1, :], 0.0), axis=1, keepdims=True)
+                 for k in range(chans)]
+        return jnp.broadcast_to(jnp.concatenate(parts, axis=0), (full, cols))
+
     for t in range(frames):
         warped_two = displaced(1, t)
         if t == 0:
@@ -302,6 +321,7 @@
                 def _():
                     for copy in w_copies(c, k):
                         copy.wait_recv()
+            biases = [bias_of(n) for n in range(1 + 2 * blocks)]
         for k in range(chans):
             @pl.when(not_me(t, k))
             def _():
@@ -319,14 +339,14 @@
         current = jnp.concatenate([L[t, r] for r in range(rows + 2 * halo)], axis=1)
         stacked = jnp.concatenate([current, warped_one, warped_two], axis=0)
         edge = halo - 1
-        joined = conv(WJ[...].reshape(9 * full, 3 * full), stacked, rows + 2 * halo, B[0])
+        joined = conv(WJ[...].reshape(9 * full, 3 * full), stacked, rows + 2 * halo, biases[0])
         state = inside([jnp.maximum(v, 0.1 * v) for v in joined], -edge)
         for n in range(blocks):
             inner = conv(W1[n].reshape(9 * full, full), jnp.concatenate(state, axis=1),
-                         rows + 2 * edge, B[1 + n])
+                         rows + 2 * edge, biases[1 + n])
             inner = inside([jnp.maximum(v, 0.0) for v in inner], 1 - edge)
             added = conv(W2[n].reshape(9 * full, full), jnp.concatenate(inner, axis=1),
-                         rows + 2 * edge - 2, B[1 + blocks + n])
+                         rows + 2 * edge - 2, biases[1 + blocks + n])
             state = inside([s.astype(jnp.float32) + v for s, v in zip(state[2:-2], added)],
                            2 - edge)
             edge -= 2
@@ -386,27 +406,27 @@
     reach = rows + halo
     full = half * chans
     lr = jnp.swapaxes(lr_feats[:, 0], 1, 2)
-    flows = jnp.stack([flow_prev[:, :, 0], flow_second[:, :, 0]], axis=1).reshape(shots, 4 * frames)
-    flows = jnp.broadcast_to(flows[:, :, None], (shots, 4 * frames, 128))
-    bias = jnp.concatenate([b_join[None], b_first, b_second], axis=0)
-    bias = jnp.broadcast_to(bias[:, :, None], bias.shape + (cols,))
+    offsets = [jnp.transpose(f[:, :, 0], (1, 2, 0)).reshape(2 * frames, shots) for f in (flow_prev, flow_second)]
+    lines = -(-(1 + 2 * blocks) // 8) * 8
     kind = lr.dtype
     dma = pltpu.SemaphoreType.DMA
     out = pl.pallas_call(
         functools.partial(plain_kernel, (frames, chans, tiles, rows, half, cols, blocks)),
         out_shape=jax.ShapeDtypeStruct((shots, rows, half, cols), kind),
-        in_specs=[pl.BlockSpec(memory_space=pltpu.VMEM)] * 6,
+        in_specs=[pl.BlockSpec(memory_space=pltpu.VMEM)] * 9,
         out_specs=pl.BlockSpec(memory_space=pltpu.VMEM),
         scratch_shapes=[
             pltpu.VMEM((frames, rows + 2 * halo, full, cols), kind),
             pltpu.VMEM((frames, rows + 2 * reach, full, cols), kind),
             pltpu.VMEM((rows + 2 * reach, full, cols), kind),
-            pltpu.VMEM((3, 4 * frames, 128), jnp.int32),
-            pltpu.SMEM((3, 4 * frames, 128), jnp.int32),
+            pltpu.VMEM((2, 2 * frames, 128), jnp.int32),
+            pltpu.VMEM((3, 2, 2 * frames, 128), jnp.int32),
+            pltpu.SMEM((3, 2, 2 * frames, 128), jnp.int32),
             pltpu.VMEM((9, full, 3 * full), kind),
             pltpu.VMEM((blocks, 9, full, full), kind),
             pltpu.VMEM((blocks, 9, full, full), kind),
-            pltpu.VMEM((1 + 2 * blocks, full, cols), jnp.float32),
+            pltpu.VMEM((lines, 128), jnp.float32),
+            pltpu.VMEM((chans, lines, 128), jnp.float32),
             dma((frames, chans, 3)), dma((frames, chans, 3)), dma((3,)), dma((3,)), dma,
             dma((chans, 4)), dma((chans, 4)), dma((frames, 5)), dma((frames, 5)),
             dma((frames, chans)), dma((shots,)),
@@ -414,7 +434,7 @@
         compiler_params=pltpu.CompilerParams(
             collective_id=0, has_side_effects=True, vmem_limit_bytes=40 * 1024 * 1024
         ),
-    )(lr, flows, w_join, w_first, w_second, bias)
+    )(lr, *offsets, w_join, w_first, w_second, b_join[None], b_first, b_second)
     return jnp.swapaxes(out, 1, 2)[:, None]
 
 
@@ -428,6 +448,8 @@
         and flow_prev.shape[2] == 1
         and halo <= rows
         and lr_feats.shape[4] == 128
+        and lr_feats.shape[2] <= 128
+        and lr_feats.shape[0] <= 128
     )
     plan = by_shots if fits else shards
     return plan(lr_feats, flow_prev, flow_second, w_join, b_join, w_first, *rest)

time: 27 us -> 25.4 us (0.941); the launches traced: 26.8 us -> 24.9 us
  Pallas kernels: 23.3 us -> 22.3 us
  local copies, waits for them, and re-layouts: 3.44 us -> 2.48 us
    pallas_call x1, Pallas kernels: 23.3 us -> 22.3 us  [by_shots(): pl.pallas_call(functools.partial(plain_kernel, (frames, chans, tiles, row...]
    unnamed x17, local copies, waits for them, and re-layouts: 2.4 us -> 1.67 us
where the time goes in v2:
time: 25.4 us; the launch traced here: 24.9 us
  Pallas kernels  22.3 us (88%)
  local copies, waits for them, and re-layouts  2.48 us (10%)
    pallas_call x1, Pallas kernels, by_shots(): pl.pallas_call(functools.partial(plain_kernel, (frames, chans, tiles, row...  22.3 us
    unnamed x17, local copies, waits for them, and re-layouts  1.67 us
    broadcast_in_dim x1, local copies, waits for them, and re-layouts, by_shots(): return jnp.swapaxes(out, 1, 2)[:, None]  0.81 us

profile of v2, /device:TPU:0, one launch (start us, length us, event | category | flops | bytes accessed | tf_op | source)
XLA Modules:
  0.0 24.9 jit_solution(11379988677595247116)
XLA Ops:
  0.0 0.0 copy-start
  0.0 0.0 copy-start.1
  0.0 0.0 copy-start.2
  0.0 0.0 copy-start.3
  0.0 0.0 copy-start.4
  0.0 1.0 %copy.13 = bf16[4,1,32,8,128]{4,2,3,0,1:T(8,128)(2,1)S(1)} copy(bf16[4,1,32,8,128]{4,3,2,1,0:T(8,128)(2,1)} %param.9) | data formatting | bytes 524288 | tf_op args[0]
  1.1 0.0 copy-start.5
  1.1 0.0 copy-start.6
  1.1 0.0 copy-start.7
  1.1 0.0 copy-done
  1.1 0.0 copy-done.1
  1.1 0.0 copy-done.2
  1.1 0.0 copy-done.3
  1.1 0.0 copy-done.4
  1.1 0.6 %copy-done.5 = f32[32]{0:T(128)S(1)} copy-done((f32[32]{0:T(128)S(1)}, f32[32]{0:T(128)}, u32[]{:S(2)}) %copy-start.5) | copy-done | bytes 152
  1.7 0.0 copy-done.6
  1.7 0.0 copy-done.7
  1.7 22.3 %shard_map.91 = bf16[4,8,32,128]{3,2,1,0:T(8,128)(2,1)S(1)} custom-call(bf16[4,8,32,128]{3,2,1,0:T(8,128)(2,1)S(1)} %bitcast.20, s32[4,4]{1,0:T(4,128)S(1)} %bitcast.21, s32[4,4]{1,0:T(4,128)S(1)} %bitcast.22, bf16[9,32,192]{2,1,0:T(8,128)(2,1)S(1)} %copy-done, bf16[1,9,32,64]{3,2,1,0:T(8,128)(2,1)S(1)} %copy-done.1, bf16[1,9,32,64]{3,2,1,0:T(8,128)(2,1)S(1)} %copy-done.2, ...), custom_call_target="tpu_custom_call" | custom-call | tf_op jit(solution)/shard_map/pallas_call | solution.py:413
  24.1 0.8 %copy.11 = bf16[4,1,32,8,128]{4,3,2,1,0:T(8,128)(2,1)} copy(bf16[4,1,32,8,128]{4,2,3,0,1:T(8,128)(2,1)S(1)} %bitcast.19) | data formatting | bytes 524288 | tf_op jit(solution)/shard_map/broadcast_in_dim | solution.py:438
Async XLA Ops:
  0.0 1.1 %copy-start = (bf16[9,32,192]{2,1,0:T(8,128)(2,1)S(1)}, bf16[9,32,192]{2,1,0:T(8,128)(2,1)}, u32[]{:S(2)}) copy-start(bf16[9,32,192]{2,1,0:T(8,128)(2,1)} %wj_ref.1) | copy-start | bytes 331780
  0.0 1.1 %copy-start.1 = (bf16[1,9,32,64]{3,2,1,0:T(8,128)(2,1)S(1)}, bf16[1,9,32,64]{3,2,1,0:T(8,128)(2,1)}, u32[]{:S(2)}) copy-start(bf16[1,9,32,64]{3,2,1,0:T(8,128)(2,1)} %w1_ref.1) | copy-start | bytes 110596
  0.0 1.1 %copy-start.2 = (bf16[1,9,32,64]{3,2,1,0:T(8,128)(2,1)S(1)}, bf16[1,9,32,64]{3,2,1,0:T(8,128)(2,1)}, u32[]{:S(2)}) copy-start(bf16[1,9,32,64]{3,2,1,0:T(8,128)(2,1)} %w2_ref.1) | copy-start | bytes 110596
  0.0 1.1 %copy-start.3 = (s32[4,2,1,2]{0,3,2,1:T(2,128)S(1)}, s32[4,2,1,2]{0,3,2,1:T(2,128)}, u32[]{:S(2)}) copy-start(s32[4,2,1,2]{0,3,2,1:T(2,128)} %param.10) | copy-start | bytes 196
  0.0 1.1 %copy-start.4 = (s32[4,2,1,2]{0,3,2,1:T(2,128)S(1)}, s32[4,2,1,2]{0,3,2,1:T(2,128)}, u32[]{:S(2)}) copy-start(s32[4,2,1,2]{0,3,2,1:T(2,128)} %param.11) | copy-start | bytes 196
  1.1 0.7 %copy-start.5 = (f32[32]{0:T(128)S(1)}, f32[32]{0:T(128)}, u32[]{:S(2)}) copy-start(f32[32]{0:T(128)} %param.13) | copy-start | bytes 388
  1.1 0.7 %copy-start.6 = (f32[1,32]{1,0:T(1,128)S(1)}, f32[1,32]{1,0:T(1,128)}, u32[]{:S(2)}) copy-start(f32[1,32]{1,0:T(1,128)} %b1_ref.1) | copy-start | bytes 388
  1.1 0.7 %copy-start.7 = (f32[1,32]{1,0:T(1,128)S(1)}, f32[1,32]{1,0:T(1,128)}, u32[]{:S(2)}) copy-start(f32[1,32]{1,0:T(1,128)} %b2_ref.1) | copy-start | bytes 388

commit v3 on v2

--- a/solution.py
+++ b/solution.py
@@ -221,12 +221,12 @@
         @pl.when(has(step))
         def _():
             fl_copy(step).start()
-    for turn in range(frames):
-        f = lax.rem(x + turn, frames)
-        for step in (0, -1, 1):
+    for step in (0, -1, 1):
+        for turn in range(frames):
+            f = lax.rem(x + frames - 1 - turn, frames)
             for k in range(chans):
                 send_lr(f, k, step)
-        if turn == 0:
+        if step == 0:
             for k in range(chans):
                 @pl.when(c != k)
                 def _():
@@ -353,7 +353,7 @@
         for r in range(rows):
             H[t, reach + r] = state[r]
         if t < frames - 1:
-            for step in (-1, 1, -2, 2):
+            for step in (-2, 2, -1, 1):
                 @pl.when(has(step))
                 def _():
                     h_copy(t, step).start()

time: 25.4 us -> 25.3 us (level); the launches traced: 24.9 us -> 25.2 us
  Pallas kernels: 22.3 us -> 22.6 us
    pallas_call x1, Pallas kernels: 22.3 us -> 22.6 us  [by_shots(): pl.pallas_call(functools.partial(plain_kernel, (frames, chans, tiles, row...]
where the time goes in v3:
time: 25.3 us; the launch traced here: 25.2 us
  Pallas kernels  22.6 us (89%)
  local copies, waits for them, and re-layouts  2.48 us (10%)
    pallas_call x1, Pallas kernels, by_shots(): pl.pallas_call(functools.partial(plain_kernel, (frames, chans, tiles, row...  22.6 us
    unnamed x17, local copies, waits for them, and re-layouts  1.67 us
    broadcast_in_dim x1, local copies, waits for them, and re-layouts, by_shots(): return jnp.swapaxes(out, 1, 2)[:, None]  0.81 us

profile of v3, /device:TPU:0, one launch (start us, length us, event | category | flops | bytes accessed | tf_op | source)
XLA Modules:
  0.0 25.2 jit_solution(9071629657086068759)
XLA Ops:
  0.0 0.0 copy-start
  0.0 0.0 copy-start.1
  0.0 0.0 copy-start.2
  0.0 0.0 copy-start.3
  0.0 0.0 copy-start.4
  0.0 1.0 %copy.13 = bf16[4,1,32,8,128]{4,2,3,0,1:T(8,128)(2,1)S(1)} copy(bf16[4,1,32,8,128]{4,3,2,1,0:T(8,128)(2,1)} %param.9) | data formatting | bytes 524288 | tf_op args[0]
  1.1 0.0 copy-start.5
  1.1 0.0 copy-start.6
  1.1 0.0 copy-start.7
  1.1 0.0 copy-done
  1.1 0.0 copy-done.1
  1.1 0.0 copy-done.2
  1.1 0.0 copy-done.3
  1.1 0.0 copy-done.4
  1.1 0.6 %copy-done.5 = f32[32]{0:T(128)S(1)} copy-done((f32[32]{0:T(128)S(1)}, f32[32]{0:T(128)}, u32[]{:S(2)}) %copy-start.5) | copy-done | bytes 152
  1.7 0.0 copy-done.6
  1.7 0.0 copy-done.7
  1.7 22.6 %shard_map.91 = bf16[4,8,32,128]{3,2,1,0:T(8,128)(2,1)S(1)} custom-call(bf16[4,8,32,128]{3,2,1,0:T(8,128)(2,1)S(1)} %bitcast.20, s32[4,4]{1,0:T(4,128)S(1)} %bitcast.21, s32[4,4]{1,0:T(4,128)S(1)} %bitcast.22, bf16[9,32,192]{2,1,0:T(8,128)(2,1)S(1)} %copy-done, bf16[1,9,32,64]{3,2,1,0:T(8,128)(2,1)S(1)} %copy-done.1, bf16[1,9,32,64]{3,2,1,0:T(8,128)(2,1)S(1)} %copy-done.2, ...), custom_call_target="tpu_custom_call" | custom-call | tf_op jit(solution)/shard_map/pallas_call | solution.py:413
  24.4 0.8 %copy.11 = bf16[4,1,32,8,128]{4,3,2,1,0:T(8,128)(2,1)} copy(bf16[4,1,32,8,128]{4,2,3,0,1:T(8,128)(2,1)S(1)} %bitcast.19) | data formatting | bytes 524288 | tf_op jit(solution)/shard_map/broadcast_in_dim | solution.py:438
Async XLA Ops:
  0.0 1.1 %copy-start = (bf16[9,32,192]{2,1,0:T(8,128)(2,1)S(1)}, bf16[9,32,192]{2,1,0:T(8,128)(2,1)}, u32[]{:S(2)}) copy-start(bf16[9,32,192]{2,1,0:T(8,128)(2,1)} %wj_ref.1) | copy-start | bytes 331780
  0.0 1.1 %copy-start.1 = (bf16[1,9,32,64]{3,2,1,0:T(8,128)(2,1)S(1)}, bf16[1,9,32,64]{3,2,1,0:T(8,128)(2,1)}, u32[]{:S(2)}) copy-start(bf16[1,9,32,64]{3,2,1,0:T(8,128)(2,1)} %w1_ref.1) | copy-start | bytes 110596
  0.0 1.1 %copy-start.2 = (bf16[1,9,32,64]{3,2,1,0:T(8,128)(2,1)S(1)}, bf16[1,9,32,64]{3,2,1,0:T(8,128)(2,1)}, u32[]{:S(2)}) copy-start(bf16[1,9,32,64]{3,2,1,0:T(8,128)(2,1)} %w2_ref.1) | copy-start | bytes 110596
  0.0 1.1 %copy-start.3 = (s32[4,2,1,2]{0,3,2,1:T(2,128)S(1)}, s32[4,2,1,2]{0,3,2,1:T(2,128)}, u32[]{:S(2)}) copy-start(s32[4,2,1,2]{0,3,2,1:T(2,128)} %param.10) | copy-start | bytes 196
  0.0 1.1 %copy-start.4 = (s32[4,2,1,2]{0,3,2,1:T(2,128)S(1)}, s32[4,2,1,2]{0,3,2,1:T(2,128)}, u32[]{:S(2)}) copy-start(s32[4,2,1,2]{0,3,2,1:T(2,128)} %param.11) | copy-start | bytes 196
  1.1 0.7 %copy-start.5 = (f32[32]{0:T(128)S(1)}, f32[32]{0:T(128)}, u32[]{:S(2)}) copy-start(f32[32]{0:T(128)} %param.13) | copy-start | bytes 388
  1.1 0.7 %copy-start.6 = (f32[1,32]{1,0:T(1,128)S(1)}, f32[1,32]{1,0:T(1,128)}, u32[]{:S(2)}) copy-start(f32[1,32]{1,0:T(1,128)} %b1_ref.1) | copy-start | bytes 388
  1.1 0.7 %copy-start.7 = (f32[1,32]{1,0:T(1,128)S(1)}, f32[1,32]{1,0:T(1,128)}, u32[]{:S(2)}) copy-start(f32[1,32]{1,0:T(1,128)} %b2_ref.1) | copy-start | bytes 388

commit v4 on v3

--- a/solution.py
+++ b/solution.py
@@ -124,8 +124,9 @@
 
 def plain_kernel(
     sizes,
-    lr_ref, fp_ref, fs_ref, wj_ref, w1_ref, w2_ref, bj_ref, b1_ref, b2_ref,
+    lr_in, fp_in, fs_in, wj_ref, w1_ref, w2_ref, bj_in, b1_in, b2_in,
     out_ref,
+    lr_got, lr_ref, fp_ref, fs_ref, bj_ref, b1_ref, b2_ref, in_sem,
     L, H, blank, FA, FL, FS, WJ, W1, W2, BA, B,
     lr_send, lr_recv, fl_send, fl_recv, fl_sem, w_send, w_recv, h_send, h_recv, o_send, o_recv,
 ):
@@ -155,6 +156,14 @@
             device_id=(clip,) + dev, device_id_type=MESH,
         )
 
+    moves = [(lr_in, lr_got), (fp_in, fp_ref), (fs_in, fs_ref), (bj_in, bj_ref), (b1_in, b1_ref),
+             (b2_in, b2_ref), (wj_ref, WJ.at[:, half_of(c)]), (w1_ref, W1.at[:, :, half_of(c)]),
+             (w2_ref, W2.at[:, :, half_of(c)])]
+    moves = [pltpu.make_async_copy(a, b, in_sem.at[n]) for n, (a, b) in enumerate(moves)]
+    loads, own_weights = moves[:6], moves[6:]
+    for copy in moves:
+        copy.start()
+
     for f in range(frames):
         for part in (slice(0, halo), slice(halo + rows, 2 * halo + rows)):
             L[f, part] = jnp.zeros((halo, full, cols), L.dtype)
@@ -163,32 +172,41 @@
     FL[...] = jnp.zeros(FL.shape, FL.dtype)
     FA[...] = jnp.zeros(FA.shape, FA.dtype)
     BA[...] = jnp.zeros(BA.shape, BA.dtype)
+
+    barrier = pltpu.get_barrier_semaphore()
+
+    def greet(dev):
+        pl.semaphore_signal(barrier, inc=1, device_id=(clip,) + dev, device_id_type=MESH)
+
+    count = len(group) - 1
+    for f, k in group:
+        @pl.when(not_me(f, k))
+        def _():
+            greet((z, f, k))
+    for step in (-1, 1):
+        for f, k in group:
+            @pl.when(has(step))
+            def _():
+                greet((z + step, f, k))
+        count = count + jnp.where(has(step), len(group), 0)
+    for step in (-2, 2):
+        @pl.when(has(step))
+        def _():
+            greet((z + step, x, c))
+        count = count + jnp.where(has(step), 1, 0)
+    for copy in loads:
+        copy.wait()
     FA[0, :, 0:frames * chans] = fp_ref[...]
     FA[1, :, 0:frames * chans] = fs_ref[...]
     for n, ref in enumerate([bj_ref] + [b1_ref.at[m:m + 1] for m in range(blocks)] + [b2_ref.at[m:m + 1] for m in range(blocks)]):
         BA[n:n + 1, 0:half] = ref[...]
-
-    barrier = pltpu.get_barrier_semaphore()
-
-    def greet(dev):
-        pl.semaphore_signal(barrier, inc=1, device_id=(clip,) + dev, device_id_type=MESH)
-
-    count = len(group) - 1
-    for f, k in group:
-        @pl.when(not_me(f, k))
-        def _():
-            greet((z, f, k))
-    for step in (-1, 1):
-        for f, k in group:
-            @pl.when(has(step))
-            def _():
-                greet((z + step, f, k))
-        count = count + jnp.where(has(step), len(group), 0)
-    for step in (-2, 2):
-        @pl.when(has(step))
-        def _():
-            greet((z + step, x, c))
-        count = count + jnp.where(has(step), 1, 0)
+    for s in range(frames * chans):
+        turned = jnp.swapaxes(lr_got[s, 0].astype(jnp.float32), 0, 1)
+        lr_ref[s] = turned.astype(lr_ref.dtype)
+    L[x, halo:halo + rows, half_of(c), :] = lr_ref[shot]
+    B[c] = BA[...]
+    FL[1] = FA[...]
+    blank[...] = jnp.zeros(blank.shape, blank.dtype)
     pl.semaphore_wait(barrier, count)
 
     span = {0: (0, rows, halo), 1: (rows - halo, halo, 0), -1: (0, halo, halo + rows)}
@@ -232,13 +250,6 @@
                 def _():
                     for copy in w_copies(k, c):
                         copy.start()
-    L[x, halo:halo + rows, half_of(c), :] = lr_ref[shot]
-    WJ[:, half_of(c), :] = wj_ref[...]
-    W1[:, :, half_of(c), :] = w1_ref[...]
-    W2[:, :, half_of(c), :] = w2_ref[...]
-    B[c] = BA[...]
-    FL[1] = FA[...]
-    blank[...] = jnp.zeros(blank.shape, blank.dtype)
     for step in (-1, 1):
         @pl.when(has(-step))
         def _():
@@ -321,6 +332,8 @@
                 def _():
                     for copy in w_copies(c, k):
                         copy.wait_recv()
+            for copy in own_weights:
+                copy.wait()
             biases = [bias_of(n) for n in range(1 + 2 * blocks)]
         for k in range(chans):
             @pl.when(not_me(t, k))
@@ -405,17 +418,25 @@
     halo = 1 + 2 * blocks
     reach = rows + halo
     full = half * chans
-    lr = jnp.swapaxes(lr_feats[:, 0], 1, 2)
     offsets = [jnp.transpose(f[:, :, 0], (1, 2, 0)).reshape(2 * frames, shots) for f in (flow_prev, flow_second)]
     lines = -(-(1 + 2 * blocks) // 8) * 8
-    kind = lr.dtype
+    kind = lr_feats.dtype
+    own_bias = (blocks, half)
     dma = pltpu.SemaphoreType.DMA
     out = pl.pallas_call(
         functools.partial(plain_kernel, (frames, chans, tiles, rows, half, cols, blocks)),
         out_shape=jax.ShapeDtypeStruct((shots, rows, half, cols), kind),
-        in_specs=[pl.BlockSpec(memory_space=pltpu.VMEM)] * 9,
+        in_specs=[pl.BlockSpec(memory_space=pltpu.HBM)] * 9,
         out_specs=pl.BlockSpec(memory_space=pltpu.VMEM),
         scratch_shapes=[
+            pltpu.VMEM(lr_feats.shape, kind),
+            pltpu.VMEM((shots, rows, half, cols), kind),
+            pltpu.VMEM((2 * frames, shots), jnp.int32),
+            pltpu.VMEM((2 * frames, shots), jnp.int32),
+            pltpu.VMEM((1, half), jnp.float32),
+            pltpu.VMEM(own_bias, jnp.float32),
+            pltpu.VMEM(own_bias, jnp.float32),
+            dma((9,)),
             pltpu.VMEM((frames, rows + 2 * halo, full, cols), kind),
             pltpu.VMEM((frames, rows + 2 * reach, full, cols), kind),
             pltpu.VMEM((rows + 2 * reach, full, cols), kind),
@@ -432,9 +453,9 @@
             dma((frames, chans)), dma((shots,)),
         ],
         compiler_params=pltpu.CompilerParams(
-            collective_id=0, has_side_effects=True, vmem_limit_bytes=40 * 1024 * 1024
+            collective_id=0, has_side_effects=True, vmem_limit_bytes=64 * 1024 * 1024
         ),
-    )(lr, *offsets, w_join, w_first, w_second, b_join[None], b_first, b_second)
+    )(lr_feats, *offsets, w_join, w_first, w_second, b_join[None], b_first, b_second)
     return jnp.swapaxes(out, 1, 2)[:, None]
 
 

time: 25.3 us -> 25.3 us (level)
  Pallas kernels: 22.6 us -> 23.4 us
  local copies, waits for them, and re-layouts: 2.48 us -> 1.76 us
    unnamed x17 -> x0, local copies, waits for them, and re-layouts: 1.67 us -> none
    broadcast_in_dim x1, local copies, waits for them, and re-layouts: 0.81 us -> 1.76 us  [by_shots(): return jnp.swapaxes(out, 1, 2)[:, None]]
    pallas_call x1, Pallas kernels: 22.6 us -> 23.4 us  [by_shots(): pl.pallas_call(functools.partial(plain_kernel, (frames, chans, tiles, row...]
where the time goes in v4:
time: 25.3 us; the launch traced here: 25.1 us
  Pallas kernels  23.4 us (92%)
  local copies, waits for them, and re-layouts  1.76 us (7%)
    pallas_call x1, Pallas kernels, by_shots(): pl.pallas_call(functools.partial(plain_kernel, (frames, chans, tiles, row...  23.4 us
    broadcast_in_dim x1, local copies, waits for them, and re-layouts, by_shots(): return jnp.swapaxes(out, 1, 2)[:, None]  1.76 us

profile of v4, /device:TPU:0, one launch (start us, length us, event | category | flops | bytes accessed | tf_op | source)
XLA Modules:
  0.0 25.1 jit_solution(7001641508469257559)
XLA Ops:
  0.0 23.4 %shard_map.91 = bf16[4,8,32,128]{3,2,1,0:T(8,128)(2,1)} custom-call(bf16[4,1,32,8,128]{4,3,2,1,0:T(8,128)(2,1)} %lr_in.1, s32[4,4]{1,0:T(4,128)} %bitcast.15, s32[4,4]{1,0:T(4,128)} %bitcast.16, bf16[9,32,192]{2,1,0:T(8,128)(2,1)} %wj_ref.1, bf16[1,9,32,64]{3,2,1,0:T(8,128)(2,1)} %w1_ref.1, bf16[1,9,32,64]{3,2,1,0:T(8,128)(2,1)} %w2_ref.1, ...), custom_call_target="tpu_custom_call" | custom-call | tf_op jit(solution)/shard_map/pallas_call | solution.py:426
  23.4 1.8 %copy.10 = bf16[4,1,32,8,128]{4,3,2,1,0:T(8,128)(2,1)} copy(bf16[4,1,32,8,128]{4,2,3,0,1:T(8,128)(2,1)} %bitcast.14) | data formatting | bytes 524288 | tf_op jit(solution)/shard_map/broadcast_in_dim | solution.py:459

commit v5 on v4

--- a/solution.py
+++ b/solution.py
@@ -453,9 +453,9 @@
             dma((frames, chans)), dma((shots,)),
         ],
         compiler_params=pltpu.CompilerParams(
-            collective_id=0, has_side_effects=True, vmem_limit_bytes=64 * 1024 * 1024
+            collective_id=0, has_side_effects=True, vmem_limit_bytes=40 * 1024 * 1024
         ),
-    )(lr_feats, *offsets, w_join, w_first, w_second, b_join[None], b_first, b_second)
+    )(*[pltpu.with_memory_space_constraint(a, pltpu.HBM) for a in (lr_feats, *offsets, w_join, w_first, w_second, b_join[None], b_first, b_second)])
     return jnp.swapaxes(out, 1, 2)[:, None]
 
 

time: 25.3 us -> 23.6 us (0.933)
  local copies, waits for them, and re-layouts: 1.76 us -> 0.81 us
  Pallas kernels: 23.4 us -> 22.7 us
    broadcast_in_dim x1, local copies, waits for them, and re-layouts: 1.76 us -> 0.81 us  [by_shots(): return jnp.swapaxes(out, 1, 2)[:, None]]
    pallas_call x1, Pallas kernels: 23.4 us -> 22.7 us  [by_shots(): pl.pallas_call(functools.partial(plain_kernel, (frames, chans, tiles, row...]
where the time goes in v5:
time: 23.6 us; the launch traced here: 23.5 us
  Pallas kernels  22.7 us (96%)
  local copies, waits for them, and re-layouts  0.81 us (3%)
    pallas_call x1, Pallas kernels, by_shots(): pl.pallas_call(functools.partial(plain_kernel, (frames, chans, tiles, row...  22.7 us
    broadcast_in_dim x1, local copies, waits for them, and re-layouts, by_shots(): return jnp.swapaxes(out, 1, 2)[:, None]  0.81 us

profile of v5, /device:TPU:0, one launch (start us, length us, event | category | flops | bytes accessed | tf_op | source)
XLA Modules:
  0.0 23.5 jit_solution(12714539263291522552)
XLA Ops:
  0.0 22.7 %shard_map.91 = bf16[4,8,32,128]{3,2,1,0:T(8,128)(2,1)S(1)} custom-call(bf16[4,1,32,8,128]{4,3,2,1,0:T(8,128)(2,1)} %lr_in.1, s32[4,4]{1,0:T(4,128)} %bitcast.15, s32[4,4]{1,0:T(4,128)} %bitcast.16, bf16[9,32,192]{2,1,0:T(8,128)(2,1)} %wj_ref.1, bf16[1,9,32,64]{3,2,1,0:T(8,128)(2,1)} %w1_ref.1, bf16[1,9,32,64]{3,2,1,0:T(8,128)(2,1)} %w2_ref.1, ...), custom_call_target="tpu_custom_call" | custom-call | tf_op jit(solution)/shard_map/pallas_call | solution.py:426
  22.7 0.8 %copy.10 = bf16[4,1,32,8,128]{4,3,2,1,0:T(8,128)(2,1)} copy(bf16[4,1,32,8,128]{4,2,3,0,1:T(8,128)(2,1)S(1)} %bitcast.14) | data formatting | bytes 524288 | tf_op jit(solution)/shard_map/broadcast_in_dim | solution.py:459
